TPU v7x, 256 devices: a whole 4x4x8 slice. The times are simulated.
256 devices in a mesh: lon: 32 (over y_hi, z, core), ch: 8 (over x, y_lo).
Axes of the slice: x: 4, y: 4 (y_hi: 2, y_lo: 2; y = y_hi * 2 + y_lo), z: 8, core: 2. Of those that a mesh axis runs over, the one named last changes fastest.
Arguments:
- field: bfloat16 [256, 1536, 128], P('lon', 'ch'), may hold values from -6 to 6
- w_query: bfloat16 [1536, 1536], P('lon', 'ch'), may hold values from -0.15625 to 0.15625
- w_key: bfloat16 [1536, 1536], P('lon', 'ch'), may hold values from -0.15625 to 0.15625
- w_value: bfloat16 [1536, 1536], P('lon', 'ch'), may hold values from -0.15625 to 0.15625
- w_proj: bfloat16 [1536, 1536], P('ch', 'lon'), may hold values from -0.15625 to 0.15625
- w_up: bfloat16 [1536, 6144], P('lon', 'ch'), may hold values from -0.15625 to 0.15625
- w_down: bfloat16 [6144, 1536], P('ch', 'lon'), may hold values from -0.078125 to 0.078125
- logit_scale: float32 [24], P('ch'), may hold values from 10 to 100
- rel_bias: float32 [24, 15, 15], P('ch'), may hold values from 0 to 16
- gain_attn: float32 [1536], P('ch'), may hold values from 0.5 to 1.5
- gain_mlp: float32 [1536], P('ch'), may hold values from 0.5 to 1.5
Outputs:
- mixed: bfloat16 [256, 1536, 128], P('lon', 'ch')
All inputs are finite; a program needn't handle non-finite values.
Results may differ from a plain program's by a relative error of at most 0.025.
Values may be sent and summed in bfloat16 or wider, within the bound.
A program may use at most 64 MiB of HBM per device.

v0:
```python
import jax
import jax.numpy as jnp
import numpy as np
from jax import lax
from jax.sharding import PartitionSpec as P

WIN = 8
SHIFT = 4


def passed_along(array, axis, by):
    count = lax.axis_size(axis)
    return lax.ppermute(array, axis, [(i, (i + by) % count) for i in range(count)])


def to_windows(array, lat, cols, heads):
    size = array.shape[1] // heads
    array = array.reshape(lat // WIN, WIN, cols // WIN, WIN, heads, size)
    return array.transpose(0, 2, 4, 1, 3, 5).reshape(
        lat // WIN, cols // WIN, heads, WIN * WIN, size
    )


def from_windows(array, lat, cols):
    heads = array.shape[2]
    size = array.shape[4]
    array = array.reshape(lat // WIN, cols // WIN, heads, WIN, WIN, size)
    return array.transpose(0, 3, 1, 4, 2, 5).reshape(lat * cols, heads * size)


def unit_rows(array):
    array = array.astype(jnp.float32)
    return (array * lax.rsqrt(jnp.sum(array * array, axis=-1, keepdims=True) + 1e-06)).astype(
        jnp.bfloat16
    )


def bias_and_mask(table, lat):
    place = np.arange(WIN * WIN)
    row_of = place // WIN
    col_of = place % WIN
    delta_row = row_of[:, None] - row_of[None, :] + WIN - 1
    delta_col = col_of[:, None] - col_of[None, :] + WIN - 1
    bias = table[:, delta_row, delta_col]
    grid_row = jnp.arange(lat // WIN)[:, None] * WIN + jnp.asarray(row_of)[None, :]
    region = grid_row >= lat - SHIFT
    allowed = region[:, :, None] == region[:, None, :]
    mask = jnp.where(allowed, 0.0, -1000000000.0).astype(jnp.float32)
    return (bias, mask)


def window_attention(query, key_in, value, scale, table, lat, cols):
    heads = scale.shape[0]
    query_w = unit_rows(to_windows(query, lat, cols, heads))
    key_w = unit_rows(to_windows(key_in, lat, cols, heads))
    value_w = to_windows(value, lat, cols, heads)
    bias, mask = bias_and_mask(table, lat)
    scores = jnp.einsum("abhid,abhjd->abhij", query_w, key_w, preferred_element_type=jnp.float32)
    scores = scores * scale[:, None, None] + bias[None, None] + mask[:, None, None]
    top = jnp.max(scores, axis=-1, keepdims=True)
    expo = jnp.exp(scores - top)
    probs = (expo / jnp.sum(expo, axis=-1, keepdims=True)).astype(jnp.bfloat16)
    out = jnp.einsum("abhij,abhjd->abhid", probs, value_w, preferred_element_type=jnp.float32)
    return from_windows(out.astype(jnp.bfloat16), lat, cols)


def normalize(resid, branch, total_one, total_two, width, gain):
    mean = total_one / width
    var = total_two / width - mean * mean
    return (resid.astype(jnp.float32) + (branch - mean) * lax.rsqrt(var + 1e-05) * gain).astype(
        jnp.bfloat16
    )


def body(
    field, w_query, w_key, w_value, w_proj, w_up, w_down, logit_scale, rel_bias, gain_attn, gain_mlp
):
    cols, local_width, lat = field.shape
    incoming = passed_along(field[:SHIFT], "lon", -1)
    moved = jnp.concatenate([field[SHIFT:], incoming], axis=0)
    shifted = jnp.roll(moved.transpose(2, 0, 1), -SHIFT, axis=0)
    count = lat * cols
    local = shifted.reshape(count, local_width)
    whole, gains_attn, gains_mlp = (
        lax.all_gather(local, "ch", axis=1, tiled=True),
        lax.all_gather(gain_attn.astype(jnp.bfloat16), "ch", axis=0, tiled=True).astype(
            gain_attn.dtype
        ),
        lax.all_gather(gain_mlp.astype(jnp.bfloat16), "ch", axis=0, tiled=True).astype(
            gain_mlp.dtype
        ),
    )
    width = whole.shape[1]
    pieces = (
        lax.all_gather(w_query, "lon", axis=0, tiled=True),
        lax.all_gather(w_key, "lon", axis=0, tiled=True),
        lax.all_gather(w_value, "lon", axis=0, tiled=True),
    )
    columns = whole
    query, key_in, value = tuple(
        (jnp.dot(columns, piece, preferred_element_type=jnp.float32) for piece in pieces)
    )
    attended = window_attention(
        query.astype(jnp.bfloat16),
        key_in.astype(jnp.bfloat16),
        value.astype(jnp.bfloat16),
        logit_scale,
        rel_bias,
        lat,
        cols,
    )
    partial_proj = jnp.dot(
        attended,
        lax.all_gather(w_proj, "lon", axis=1, tiled=True),
        preferred_element_type=jnp.float32,
    )
    mine = lax.psum_scatter(
        partial_proj.astype(jnp.bfloat16), "ch", scatter_dimension=1, tiled=True
    ).astype(jnp.float32)
    one, two = lax.psum(
        (jnp.sum(mine, axis=1, keepdims=True), jnp.sum(mine * mine, axis=1, keepdims=True)), "ch"
    )
    after = normalize(local, mine, one, two, width, gain_attn)
    mlp_in = lax.all_gather(after, "ch", axis=1, tiled=True)
    columns = mlp_in
    up_sum = jnp.dot(
        columns, lax.all_gather(w_up, "lon", axis=0, tiled=True), preferred_element_type=jnp.float32
    )
    hidden = jax.nn.gelu(up_sum, approximate=False).astype(jnp.bfloat16)
    partial_down = jnp.dot(
        hidden,
        lax.all_gather(w_down, "lon", axis=1, tiled=True),
        preferred_element_type=jnp.float32,
    )
    down = lax.psum_scatter(
        partial_down.astype(jnp.bfloat16), "ch", scatter_dimension=1, tiled=True
    ).astype(jnp.float32)
    one_m, two_m = lax.psum(
        (jnp.sum(down, axis=1, keepdims=True), jnp.sum(down * down, axis=1, keepdims=True)), "ch"
    )
    block = normalize(after, down, one_m, two_m, width, gain_mlp).reshape(lat, cols, local_width)
    block = jnp.roll(block, SHIFT, axis=0).transpose(1, 2, 0)
    outgoing = passed_along(block[cols - SHIFT :], "lon", 1)
    return jnp.concatenate([outgoing, block[: cols - SHIFT]], axis=0)


def solution(mesh):
    placed = (
        P("lon", "ch", None),
        P("lon", "ch"),
        P("lon", "ch"),
        P("lon", "ch"),
        P("ch", "lon"),
        P("lon", "ch"),
        P("ch", "lon"),
        P("ch"),
        P("ch", None, None),
        P("ch"),
        P("ch"),
    )
    return jax.shard_map(
        body, mesh=mesh, in_specs=placed, out_specs=P("lon", "ch", None), check_vma=False
    )
```

profile of v0, /device:TPU:1, one launch (start us, length us, event | category | flops | bytes accessed | tf_op | source)
XLA Modules:
  0.0 644.3 jit_solution(5558665080902452925)
XLA Ops:
  7.4 1.1 fusion.97
  8.4 3.3 collective-permute-start
  11.8 3.1 collective-permute-done
  15.8 0.9 copy.46
  17.0 25.6 %gather_fusion = f32[4096,3]{1,0:T(8,128)S(1)} fusion(f32[3,15,15]{0,2,1:T(8,128)S(1)} %copy.58, s32[4096]{0:T(1024)S(1)} %copy-done), kind=kCustom, calls=%fused_computation | custom fusion | bytes 131072 | tf_op jit(solution)/shard_map/gather | solution.py:44
  42.6 1.2 copy.59
  43.8 1.0 compare_select_fusion
  44.9 47.0 %all_gather.25 = bf16[1536,192]{1,0:T(8,128)(2,1)S(1)} all-gather(bf16[48,192]{1,0:T(8,128)(2,1)S(1)} %copy-done.7), channel_id=1, replica_groups=mesh['lon'=32,'ch'=8] {'lon'}, dimensions={0}, use_global_device_ids=true | all-gather | bytes 608256 | tf_op jit(solution)/shard_map/all_gather | solution.py:95
  91.9 42.6 %all_gather.26 = bf16[1536,192]{1,0:T(8,128)(2,1)} all-gather(bf16[48,192]{1,0:T(8,128)(2,1)S(1)} %copy-done.8), channel_id=1, replica_groups=mesh['lon'=32,'ch'=8] {'lon'}, dimensions={0}, use_global_device_ids=true | all-gather | bytes 608256 | tf_op jit(solution)/shard_map/all_gather | solution.py:96
  134.5 42.0 %all_gather.27 = bf16[1536,192]{1,0:T(8,128)(2,1)} all-gather(bf16[48,192]{1,0:T(8,128)(2,1)S(1)} %copy-done.9), channel_id=1, replica_groups=mesh['lon'=32,'ch'=8] {'lon'}, dimensions={0}, use_global_device_ids=true | all-gather | bytes 608256 | tf_op jit(solution)/shard_map/all_gather | solution.py:97
  176.5 42.3 %all_gather.28 = bf16[192,1536]{0,1:T(8,128)(2,1)} all-gather(bf16[192,48]{0,1:T(8,128)(2,1)S(1)} %copy-done.10), channel_id=1, replica_groups=mesh['lon'=32,'ch'=8] {'lon'}, dimensions={1}, use_global_device_ids=true | all-gather | bytes 608256 | tf_op jit(solution)/shard_map/all_gather | solution.py:114
  218.8 3.7 fusion.99
  222.5 1.3 copy.49
  223.8 3.6 mul.123
  227.4 3.6 reduce_sum.63
  231.0 1.9 rsqrt_bitcast_fusion.1
  232.9 1.3 copy.51
  234.2 3.1 fusion.98
  237.3 2.5 copy.54
  239.8 3.4 mul.127
  243.2 3.6 reduce_sum.64
  246.8 1.9 rsqrt_bitcast_fusion
  248.7 1.3 copy.56
  250.0 2.5 copy.48
  252.5 3.4 reshape.188
  255.9 2.4 copy.53
  258.4 3.4 reshape.189
  261.8 3.4 add_add_fusion
  265.2 1.1 fusion.100
  266.4 0.8 convolution_convert_fusion.3
  267.8 2.5 fusion.46
  270.3 1.1 copy.83
  271.4 0.7 reshape.185
  272.1 2.7 convolution_convert_fusion
  276.0 73.2 %reduce-scatter.3.cloned.1.call-done = bf16[1024,192]{0,1:T(8,128)(2,1)} async-done(((bf16[1024,1536]{0,1:T(8,128)(2,1)}), bf16[1024,192]{0,1:T(8,128)(2,1)}) %reduce-scatter.3.cloned.1.call-update) | async-done | bytes 393232 | tf_op jit(solution)/shard_map/reduce_scatter | solution.py:117
  349.2 1.1 convert_reduce_fusion.1
  350.3 15.4 %all-reduce.1 = (f32[1024,1]{0,1:T(1,128)S(1)}, f32[1024,1]{0,1:T(1,128)S(1)}) all-reduce(f32[1024,1]{0,1:T(1,128)S(1)} %bitcast.68, f32[1024,1]{0,1:T(1,128)S(1)} %bitcast.67), channel_id=1, replica_groups=mesh['lon'=32,'ch'=8] {'ch'}, use_global_device_ids=true, to_apply=%region_8.9 | all-reduce | flops 2048 | bytes 16384 | tf_op jit(solution)/shard_map/psum | solution.py:120
  365.8 1.9 fusion.52
  368.4 79.9 %all-gather.9.cloned.1.call-done = bf16[1536,768]{1,0:T(8,128)(2,1)} async-done(((bf16[48,768]{1,0:T(8,128)(2,1)}), bf16[1536,768]{1,0:T(8,128)(2,1)}) %all-gather.9.cloned.1.call-update) | async-done | bytes 2359312 | tf_op jit(solution)/shard_map/all_gather | solution.py:127
  448.3 70.6 %all-gather.7.cloned.1.call-done = bf16[1024,1536]{0,1:T(8,128)(2,1)} async-done(((bf16[1024,192]{0,1:T(8,128)(2,1)}), bf16[1024,1536]{0,1:T(8,128)(2,1)}) %all-gather.7.cloned.1.call-update) | async-done | bytes 3145744 | tf_op jit(solution)/shard_map/all_gather | solution.py:124
  518.8 14.9 %convolution_convert_fusion.1 = bf16[1024,1536]{0,1:T(8,128)(2,1)} fusion(bf16[768,1536]{0,1:T(8,128)(2,1)} %all-gather.11.cloned.1.call-done, bf16[1024,1536]{0,1:T(8,128)(2,1)} %all-gather.7.cloned.1.call-done, bf16[1536,768]{1,0:T(8,128)(2,1)} %all-gather.9.cloned.1.call-done), kind=kOutput, calls=%fused_computation.4 | convolution fusion | flops 4884529152 | bytes 11010048 | tf_op jit(solution)/shard_map/dot_general | solution.py:130
  533.8 74.0 %reduce-scatter.5.cloned.1.call-done = bf16[1024,192]{0,1:T(8,128)(2,1)} async-done(((bf16[1024,1536]{0,1:T(8,128)(2,1)}), bf16[1024,192]{0,1:T(8,128)(2,1)}) %reduce-scatter.5.cloned.1.call-update) | async-done | bytes 393232 | tf_op jit(solution)/shard_map/reduce_scatter | solution.py:135
  607.8 1.1 convert_reduce_fusion
  608.9 15.7 %all-reduce = (f32[1024,1]{0,1:T(1,128)S(1)}, f32[1024,1]{0,1:T(1,128)S(1)}) all-reduce(f32[1024,1]{0,1:T(1,128)S(1)} %bitcast.70, f32[1024,1]{0,1:T(1,128)S(1)} %bitcast.69), channel_id=1, replica_groups=mesh['lon'=32,'ch'=8] {'ch'}, use_global_device_ids=true, to_apply=%region_13.14 | all-reduce | flops 2048 | bytes 16384 | tf_op jit(solution)/shard_map/psum | solution.py:138
  624.7 1.2 fusion.57
  626.5 5.7 collective-permute-start.1
  632.2 3.3 collective-permute-done.1
  635.8 1.1 copy.66
  (63 shorter events, 4.6 us)
Async XLA Ops:
  7.4 9.6 %copy-start = (s32[4096]{0:T(1024)S(1)}, s32[4096]{0:T(1024)}, u32[]{:S(2)}) copy-start(s32[4096]{0:T(1024)} %constant.125) | copy-start | bytes 49156
  7.4 9.4 %copy-start.11 = (f32[3,15,15]{2,1,0:T(8,128)S(1)}, f32[3,15,15]{2,1,0:T(8,128)}, u32[]{:S(2)}) copy-start(f32[3,15,15]{2,1,0:T(8,128)} %param.24) | copy-start | bytes 8104
  7.4 211.4 %all-gather.5.cloned.1.call-start = ((), (), s32[]{:S(2)}) async-start(), calls=%async_computation.2 | async-start | bytes 3538944 | tf_op jit(solution)/shard_map/all_gather | solution.py:85
  8.4 6.5 %collective-permute-start = (bf16[4,192,128]{2,1,0:T(8,128)(2,1)S(1)}, bf16[4,192,128]{2,1,0:T(8,128)(2,1)S(1)}, u32[]{:S(2)}, u32[]{:S(2)}) collective-permute-start(bf16[4,192,128]{2,1,0:T(8,128)(2,1)S(1)} %get-tuple-element.16), channel_id=1, source_target_pairs={{0,248},{8,0},{16,8},{24,16},{32,24},{40,32},{48,40},{56,48},{64,5... | collective-permute-start | bytes 589832 | tf_op jit(solution)/shard_map/ppermute | solution.py:13
  15.8 28.0 %copy-start.15 = (s32[64]{0:T(128)S(1)}, s32[64]{0:T(128)}, u32[]{:S(2)}) copy-start(s32[64]{0:T(128)} %constant.92.clone) | copy-start | bytes 772
  16.7 28.1 %copy-start.7 = (bf16[48,192]{1,0:T(8,128)(2,1)S(1)}, bf16[48,192]{1,0:T(8,128)(2,1)}, u32[]{:S(2)}) copy-start(bf16[48,192]{1,0:T(8,128)(2,1)} %param.17) | copy-start | bytes 55300
  16.7 332.5 %reduce-scatter.3.cloned.1.call-start = ((), (), s32[]{:S(2)}) async-start(), calls=%async_computation.3 | async-start | bytes 3538944 | tf_op jit(solution)/shard_map/reduce_scatter | solution.py:117
  17.0 74.9 %copy-start.8 = (bf16[48,192]{1,0:T(8,128)(2,1)S(1)}, bf16[48,192]{1,0:T(8,128)(2,1)}, u32[]{:S(2)}) copy-start(bf16[48,192]{1,0:T(8,128)(2,1)} %param.18) | copy-start | bytes 55300
  17.0 117.5 %copy-start.9 = (bf16[48,192]{1,0:T(8,128)(2,1)S(1)}, bf16[48,192]{1,0:T(8,128)(2,1)}, u32[]{:S(2)}) copy-start(bf16[48,192]{1,0:T(8,128)(2,1)} %param.19) | copy-start | bytes 55300
  42.6 133.9 %copy-start.10 = (bf16[192,48]{0,1:T(8,128)(2,1)S(1)}, bf16[192,48]{0,1:T(8,128)(2,1)}, u32[]{:S(2)}) copy-start(bf16[192,48]{0,1:T(8,128)(2,1)} %param.20) | copy-start | bytes 55300
  223.8 10.3 %copy-start.1 = (bf16[1024,1536]{0,1:T(8,128)(2,1)S(1)}, bf16[1024,1536]{0,1:T(8,128)(2,1)}, u32[]{:S(2)}) copy-start(bf16[1024,1536]{0,1:T(8,128)(2,1)} %all-gather.5.cloned.1.call-done) | copy-start | bytes 9437188
  255.9 5.9 copy-start.14
  261.8 4.6 copy-start.6
  265.2 1.2 copy-start.5
  270.3 1.8 copy-start.4
  274.7 91.1 %copy-start.2 = (bf16[1024,192]{0,1:T(8,128)(2,1)S(1)}, bf16[1024,192]{0,1:T(8,128)(2,1)}, u32[]{:S(2)}) copy-start(bf16[1024,192]{0,1:T(8,128)(2,1)} %copy.46) | copy-start | bytes 1179652
  274.7 91.1 %copy-start.12 = (f32[192]{0:T(256)S(1)}, f32[192]{0:T(256)}, u32[]{:S(2)}) copy-start(f32[192]{0:T(256)} %param.25) | copy-start | bytes 2308
  274.8 93.6 %all-gather.11.cloned.1.call-start = ((), (), s32[]{:S(2)}) async-start(), calls=%async_computation.6 | async-start | bytes 2433024 | tf_op jit(solution)/shard_map/all_gather | solution.py:132
  275.3 172.9 %all-gather.9.cloned.1.call-start = ((), (), s32[]{:S(2)}) async-start(), calls=%async_computation.5 | async-start | bytes 2433024 | tf_op jit(solution)/shard_map/all_gather | solution.py:127
  275.9 242.9 %all-gather.7.cloned.1.call-start = ((), (), s32[]{:S(2)}) async-start(), calls=%async_computation.4 | async-start | bytes 3538944 | tf_op jit(solution)/shard_map/all_gather | solution.py:124
  367.8 240.0 %reduce-scatter.5.cloned.1.call-start = ((), (), s32[]{:S(2)}) async-start(), calls=%async_computation.7 | async-start | bytes 3538944 | tf_op jit(solution)/shard_map/reduce_scatter | solution.py:135
  533.7 90.9 %copy-start.3 = (bf16[1024,192]{0,1:T(8,128)(2,1)S(1)}, bf16[1024,192]{0,1:T(8,128)(2,1)}, u32[]{:S(2)}) copy-start(bf16[1024,192]{0,1:T(8,128)(2,1)} %fusion.52) | copy-start | bytes 1179652
  533.7 90.9 %copy-start.13 = (f32[192]{0:T(256)S(1)}, f32[192]{0:T(256)}, u32[]{:S(2)}) copy-start(f32[192]{0:T(256)} %param.26) | copy-start | bytes 2308
  626.5 9.0 %collective-permute-start.1 = (bf16[4,192,128]{1,0,2:T(4,128)(2,1)S(1)}, bf16[4,192,128]{1,0,2:T(4,128)(2,1)S(1)}, u32[]{:S(2)}, u32[]{:S(2)}) collective-permute-start(bf16[4,192,128]{1,0,2:T(4,128)(2,1)S(1)} %get-tuple-element.13), channel_id=1, source_target_pairs={{0,8},{8,16},{16,24},{24,32},{32,40},{40,48},{48,56},{56,64},{64,7... | collective-permute-start | bytes 589832 | tf_op jit(solution)/shard_map/ppermute | solution.py:13
Sparse Core Ops, SparseCore 0:
  16.9 81.0 all-gather.4
  274.9 74.2 reduce-scatter.2
  533.9 73.8 reduce-scatter.4
Sparse Core Ops, SparseCore 1:
  278.0 90.3 all-gather.10
  371.0 77.2 all-gather.8
  449.9 68.8 all-gather.6
where the time goes:
time: 648 us; the launch traced here: 644 us
  waiting for transfers between devices  306 us (47%)
  blocking collectives  205 us (32%)
  local copies, waits for them, and re-layouts  58.6 us (9%)
  matrix products  31.2 us (5%)
  other arithmetic  19.3 us (3%)
  between operations  15.1 us (2%)
  starting transfers between devices  9.23 us (1%)
    all_gather x1, waiting for transfers between devices, body(): lax.all_gather(w_up, 'lon', axis=0, tiled=True)  79.9 us
    reduce_scatter x1, waiting for transfers between devices, body(): lax.psum_scatter(partial_down.astype(jnp.bfloat16), 'ch', scatter_dimensi...  74 us
    reduce_scatter x1, waiting for transfers between devices, body(): lax.psum_scatter(partial_proj.astype(jnp.bfloat16), 'ch', scatter_dimensi...  73.2 us
    all_gather x1, waiting for transfers between devices, body(): mlp_in = lax.all_gather(after, 'ch', axis=1, tiled=True)  70.6 us
    all_gather x1, blocking collectives, body(): lax.all_gather(w_query, 'lon', axis=0, tiled=True)  47 us
    all_gather x1, blocking collectives, body(): lax.all_gather(w_key, 'lon', axis=0, tiled=True)  42.6 us
    all_gather x1, blocking collectives, body(): lax.all_gather(w_proj, 'lon', axis=1, tiled=True)  42.3 us
    all_gather x1, blocking collectives, body(): lax.all_gather(w_value, 'lon', axis=0, tiled=True)  42 us
  transfers between devices with their start and end apart: 8, of which 7 were waited for; matrix products, arithmetic and copies ran while one was open for 5% of the time, Pallas kernels for 0%

commit v1 on v0

v1 whole, which is shorter than its diff:
```python
import functools

import jax
import jax.numpy as jnp
from jax import lax
from jax.experimental import pallas as pl
from jax.experimental.pallas import tpu as pltpu
from jax.sharding import PartitionSpec as P

MESH = pl.DeviceIdType.MESH
BF = jnp.bfloat16
F32 = jnp.float32
D = 1536
NX, NY, NZ = 4, 4, 8
ROWS = 48
PACK = 768
TOK = 256
PART = 192
PIECE = 384
NCHUNK = 2
SEMS = 160


def nt(a, b):
    return lax.dot_general(a, b, (((1,), (1,)), ((), ())), preferred_element_type=F32)


def nn(a, b):
    return jnp.dot(a, b, preferred_element_type=F32)


def gelu(v):
    return 0.5 * v * (1.0 + lax.erf(v * 0.7071067811865476))


def kernel(
    blk, wp, aux, gain, out,
    gw, rin, xf, qs, at, pb, rp, af, hs, db, rd, ss, st, ga, ea, bias, ob,
    send, recv,
):
    lon = lax.axis_index("lon")
    ch = lax.axis_index("ch")
    x, yl = ch // 2, ch % 2
    core, z, yh = lon % 2, (lon // 2) % NZ, lon // (2 * NZ)
    y = yh * 2 + yl

    def at_x(dx):
        return (lon, ((x + dx) % NX) * 2 + yl)

    def at_z(dz):
        return ((yh * NZ + (z + dz) % NZ) * 2 + core, ch)

    def at_y(dy):
        yy = (y + dy) % NY
        return (((yy // 2) * NZ + z) * 2 + core, x * 2 + yy % 2)

    sibling = (lon + 1 - 2 * core, ch)
    partner = (lon, x * 2 + 1 - yl)

    def at_lon(dl, other):
        c = x * 2 + 1 - yl if other else ch
        return ((lon + dl) % 32, c)

    def peer(dx, other):
        c = 1 - yl if other else yl
        return (lon, ((x + dx) % NX) * 2 + c)

    peers = [(1, 0), (3, 0), (2, 0), (0, 1), (1, 1), (3, 1), (2, 1)]

    barrier = pltpu.get_barrier_semaphore()
    greeted = [peer(a, b) for a, b in peers]
    greeted += [at_z(1), at_z(-1), at_y(1), at_y(-1), sibling]
    greeted += [at_lon(1, 0), at_lon(1, 1), at_lon(-1, 0), at_lon(-1, 1)]
    for device in greeted:
        pl.semaphore_signal(barrier, inc=1, device_id=device, device_id_type=MESH)
    pl.semaphore_wait(barrier, len(greeted))

    started = []

    def push(src, dst, device):
        k = len(started)
        copy = pltpu.make_async_remote_copy(
            src_ref=src, dst_ref=dst, send_sem=send.at[k], recv_sem=recv.at[k],
            device_id=device, device_id_type=MESH,
        )
        copy.start()
        started.append(copy)
        return copy

    def wblock(t, yy, zz):
        return gw.at[t, yy % 2, yy // 2, zz % NZ, core]

    zc, yc, yr, dc = {}, {}, {}, {}

    def z_send(t, s):
        if s < 4:
            ref = wblock(t, y, z - s + 1 + NZ)
            zc[t, s, 1] = push(ref, ref, at_z(1))
            ref = wblock(t, y, z + s - 1)
            zc[t, s, -1] = push(ref, ref, at_z(-1))
        else:
            sign = -1 if t == 1 else 1
            ref = wblock(t, y, z - sign * 3 + NZ)
            zc[t, s, sign] = push(ref, ref, at_z(sign))

    def z_wait(t, s):
        for sign in (1, -1):
            if (t, s, sign) in zc:
                zc[t, s, sign].wait_recv()

    ORDER = [0, 1, -1, 2, -2, 3, -3, 4]

    def y_send_one(t, k):
        ref = wblock(t, y, z + ORDER[k] + NZ)
        yc[t, k, 1] = push(ref, ref, at_y(1))
        yc[t, k, -1] = push(ref, ref, at_y(-1))

    def y_relay_one(t, k):
        yc[t, k, 1].wait_recv()
        yc[t, k, -1].wait_recv()
        sign = 1 if k % 2 == 0 else -1
        ref = wblock(t, (y - sign + NY) % NY, z + ORDER[k] + NZ)
        yr[t, k] = push(ref, ref, at_y(sign))

    def group(t, yy, lo=0, size=NZ):
        yy = (yy + NY) % NY
        return gw.at[t, yy % 2, yy // 2, pl.ds(lo, size), core]

    def y_send_all(t):
        ref = group(t, y)
        yc[t, 1] = push(ref, ref, at_y(1))
        yc[t, -1] = push(ref, ref, at_y(-1))

    def y_relay_all(t):
        yc[t, 1].wait_recv()
        yc[t, -1].wait_recv()
        ref = group(t, y - 1, 0, 4)
        yr[t, 0] = push(ref, ref, at_y(1))
        ref = group(t, y + 1, 4, 4)
        yr[t, 1] = push(ref, ref, at_y(-1))

    def to_sibling(t, dy):
        ref = group(t, y + dy)
        dc[t, dy] = push(ref, ref, sibling)

    def sibling_wait(t):
        for dy in (0, 1, -1, 2):
            dc[t, dy].wait_recv()

    rows_mine = pl.ds(pl.multiple_of(yl * PART, PART), PART)
    ic = {}

    def input_send(g):
        for name, src, cg, device in (
            ("partner", blk.at[1 - yl, g, 1], 0, partner),
            ("west", blk.at[yl, g, 0], 1, at_lon(31, 0)),
            ("both", blk.at[1 - yl, g, 0], 1, at_lon(31, 1)),
        ):
            ic[g, name] = push(src, rin.at[g, cg, rows_mine], device)

    for t in range(3):
        gw[t, yl, yh, z, core] = wp[t]
    input_send(0)
    z_send(0, 1)
    input_send(1)
    y_send_one(0, 0)
    ea[yl] = aux[...]
    aux_copy = push(ea.at[yl], ea.at[yl], partner)
    lanes_mine = pl.ds(pl.multiple_of(x * PIECE, 128), PIECE)
    ga[yl, :, lanes_mine] = gain[...]
    gain_copies = [
        push(ga.at[yl, :, lanes_mine], ga.at[yl, :, lanes_mine], peer(a, b)) for a, b in peers
    ]

    xc, xr = {}, {}

    def x_send(g):
        for cp in ("partner", "west", "both"):
            ic[g, cp].wait_recv()
        rin[g, 0, rows_mine] = blk[yl, g, 1]
        for cg in range(2):
            piece = rin[g, cg].astype(F32).T.astype(BF)
            xf[g, pl.ds(cg * 128, 128), lanes_mine] = piece
        ref = xf.at[g, :, lanes_mine]
        xc[g, 1] = push(ref, ref, at_x(1))
        xc[g, -1] = push(ref, ref, at_x(3))

    def x_relay(g):
        for sign, half in ((1, 0), (-1, 1)):
            xc[g, sign].wait_recv()
            lanes = pl.ds(pl.multiple_of(((x + 4 - sign) % NX) * PIECE, 128), PIECE)
            ref = xf.at[g, pl.ds(half * 128, 128), lanes]
            xr[g, sign] = push(ref, ref, at_x(sign + 4))

    z_wait(0, 1)
    z_send(0, 2)
    x_send(0)
    y_send_one(0, 1)
    y_send_one(0, 2)
    z_wait(0, 2)
    z_send(0, 3)
    x_send(1)
    y_send_one(0, 3)
    y_send_one(0, 4)
    z_wait(0, 3)
    z_send(0, 4)
    y_send_one(0, 5)
    y_send_one(0, 6)
    z_send(1, 1)
    x_relay(0)
    y_relay_one(0, 0)
    z_wait(0, 4)
    y_send_one(0, 7)
    to_sibling(0, 0)
    z_wait(1, 1)
    z_send(1, 2)
    y_relay_one(0, 1)
    y_relay_one(0, 2)
    z_wait(1, 2)
    z_send(1, 3)
    y_relay_one(0, 3)
    x_relay(1)
    y_relay_one(0, 4)
    z_wait(1, 3)
    z_send(1, 4)
    y_relay_one(0, 5)
    y_relay_one(0, 6)
    y_relay_one(0, 7)
    to_sibling(0, 1)
    to_sibling(0, -1)
    z_send(2, 1)
    z_wait(1, 4)
    to_sibling(1, 0)
    y_send_all(1)
    z_wait(2, 1)
    z_send(2, 2)

    aux_copy.wait_recv()
    for part in range(2):
        for h in range(3):
            table = ea[part, h]
            for ci in range(8):
                bias[part, h, pl.ds(ci * 8, 8), :] = table[:, (7 - ci) * 8:(7 - ci) * 8 + 64]
    z_wait(2, 2)
    z_send(2, 3)
    for k in range(8):
        yr[0, k].wait_recv()
    to_sibling(0, 2)
    z_wait(2, 3)
    z_send(2, 4)
    sibling_wait(0)
    z_wait(2, 4)
    to_sibling(2, 0)

    row_i = lax.broadcasted_iota(jnp.int32, (64, 64), 0) % 8
    row_j = lax.broadcasted_iota(jnp.int32, (64, 64), 1) % 8
    poles = jnp.where((row_i >= 4) != (row_j >= 4), -1e9, 0.0).astype(F32)

    def unit(v):
        return (v * lax.rsqrt(jnp.sum(v * v, axis=-1, keepdims=True) + 1e-6)).astype(BF)

    pc = {}

    def attention(g):
        xr[g, 1].wait_recv()
        xr[g, -1].wait_recv()
        for part in range(2):
            for lo, size in ((0, 256), (256, 256), (512, 128)):
                w = gw[0, part, :, :, :, :, lo:lo + size].reshape(D, size)
                r = nn(xf[g], w).astype(BF).astype(F32)
                qs[part, :, :, lo:lo + size] = r.reshape(8, 32, size)

        def window(w, carry):
            lat = pl.ds(pl.multiple_of(w * 8, 8), 8)
            last = jnp.logical_and(yl == 1, w == 3) if g == NCHUNK - 1 else None
            for part in range(2):
                qkv = qs[part, :, lat, :].reshape(64, 640)
                heads = [jnp.zeros((64, 64), F32)]
                for h in range(3):
                    q = unit(qkv[:, h * 64:h * 64 + 64])
                    k = unit(qkv[:, 192 + h * 64:256 + h * 64])
                    v = qkv[:, 384 + h * 64:448 + h * 64].astype(BF)
                    s = nt(q, k) * ea[part, 3 + h, 0:1, 0:1] + bias[part, h]
                    if last is not None:
                        s = s + jnp.where(last, poles, 0.0)
                    e = jnp.exp(s - jnp.max(s, axis=-1, keepdims=True))
                    p = (e / jnp.sum(e, axis=-1, keepdims=True)).astype(BF)
                    heads.append(nn(p, v))
                o = jnp.concatenate(heads, axis=1)
                at[:, lat, part * 256:part * 256 + 256] = o.reshape(8, 8, 256)
            return carry

        lax.fori_loop(0, 4, window, 0)

        a = at[...].reshape(TOK, 512).astype(BF)

        def columns(n, carry):
            total = jnp.zeros((TOK, PIECE), F32)
            for part in range(2):
                w = gw[0, part, n // 2, pl.ds((n % 2) * 4, 4), :, :, 512:768].reshape(PIECE, 256)
                total = total + nt(a[:, part * 256:part * 256 + 256], w)
            lanes = pl.ds(pl.multiple_of(n * PIECE, 128), PIECE)
            pb[g, :, lanes] = total.astype(BF)
            return carry

        lax.fori_loop(0, 4, columns, 0)
        for slot, dx in ((0, 2), (1, 1), (2, 3)):
            rows = pl.ds(pl.multiple_of(((x + dx) % NX) * 64, 64), 64)
            pc[g, slot] = push(pb.at[g, rows], rp.at[g, slot], at_x(dx))

    ac, ar = {}, {}
    my_rows = pl.ds(pl.multiple_of(x * 64, 64), 64)

    def norm_one(g):
        for slot in range(3):
            pc[g, slot].wait_recv()
        v = pb[g, my_rows, :].astype(F32)
        for slot in range(3):
            v = v + rp[g, slot].astype(F32)
        mean = jnp.sum(v, axis=1, keepdims=True) * (1.0 / D)
        var = jnp.sum(v * v, axis=1, keepdims=True) * (1.0 / D) - mean * mean
        gains = ga[0, 0:1, :] + ga[1, 0:1, :]
        res = xf[g, my_rows, :].astype(F32)
        af[g, my_rows, :] = (res + (v - mean) * lax.rsqrt(var + 1e-5) * gains).astype(BF)
        ref = af.at[g, my_rows]
        ac[g, 1] = push(ref, ref, at_x(1))
        ac[g, -1] = push(ref, ref, at_x(3))

    def a_relay(g):
        for sign, half in ((1, 0), (-1, 1)):
            ac[g, sign].wait_recv()
            start = ((x + 4 - sign) % NX) * 64 + half * 32
            ref = af.at[g, pl.ds(pl.multiple_of(start, 32), 32)]
            ar[g, sign] = push(ref, ref, at_x(sign + 4))

    def up(g):
        ar[g, 1].wait_recv()
        ar[g, -1].wait_recv()

        def columns(n, carry):
            lo = pl.multiple_of((n % 3) * 256, 256)
            w = gw[1, n // 3, :, :, :, :, pl.ds(lo, 256)].reshape(D, 256)
            hs[:, pl.ds(pl.multiple_of(n * 256, 256), 256)] = gelu(nn(af[g], w)).astype(BF)
            return carry

        lax.fori_loop(0, 6, columns, 0)

    rc = {}

    def down(g):
        for slot, dx in ((0, 2), (1, 1), (2, 3), (3, 0)):
            xx = (x + dx) % NX
            total = jnp.zeros((PIECE, TOK), F32)
            for part in range(2):
                w = gw[2, part, xx // 2, pl.ds((xx % 2) * 4, 4)].reshape(PIECE, PACK)
                total = total + nt(w, hs[:, part * PACK:part * PACK + PACK])
            db[g, slot] = total.astype(BF)
            if slot < 3:
                rc[g, slot] = push(db.at[g, slot], rd.at[g, slot], at_x(dx))

    sc = {}

    def stats(g):
        for slot in range(3):
            rc[g, slot].wait_recv()
        v = db[g, 3].astype(F32)
        for slot in range(3):
            v = v + rd[g, slot].astype(F32)
        one = jnp.sum(v, axis=0, keepdims=True)
        two = jnp.sum(v * v, axis=0, keepdims=True)
        ss[g, 0:1, :] = one
        ss[g, 1:2, :] = two
        for slot, dx in ((0, 2), (1, 1), (2, 3)):
            sc[g, slot] = push(ss.at[g], st.at[g, slot], at_x(dx))
        return v

    oc = []

    def final(g, v):
        res = af[g, :, lanes_mine].astype(F32).T
        row = ga[0, 1:2, lanes_mine] + ga[1, 1:2, lanes_mine]
        col = jnp.broadcast_to(row, (128, PIECE)).T
        gains = jnp.concatenate([col, col], axis=1)
        for slot in range(3):
            sc[g, slot].wait_recv()
        tot = ss[g] + st[g, 0] + st[g, 1] + st[g, 2]
        mean = tot[0:1] * (1.0 / D)
        var = tot[1:2] * (1.0 / D) - mean * mean
        o = (res + (v - mean) * lax.rsqrt(var + 1e-5) * gains).astype(BF)
        for cg in range(2):
            ob[g, cg] = o[:, cg * 128:cg * 128 + 128].reshape(2, PART, 128)
        out[yl, g, 1] = ob[g, 0, yl]
        for src, half, device in (
            (ob.at[g, 0, 1 - yl], 1, partner),
            (ob.at[g, 1, yl], 0, at_lon(1, 0)),
            (ob.at[g, 1, 1 - yl], 0, at_lon(1, 1)),
        ):
            oc.append(push(src, out.at[yl, g, half], device))

    ss[...] = jnp.zeros_like(ss)
    attention(0)
    y_relay_all(1)
    to_sibling(1, 1)
    to_sibling(1, -1)
    y_send_all(2)
    attention(1)
    for cp in gain_copies:
        cp.wait_recv()
    norm_one(0)
    yr[1, 0].wait_recv()
    yr[1, 1].wait_recv()
    to_sibling(1, 2)
    y_relay_all(2)
    to_sibling(2, 1)
    to_sibling(2, -1)
    a_relay(0)
    norm_one(1)
    sibling_wait(1)
    up(0)
    a_relay(1)
    yr[2, 0].wait_recv()
    yr[2, 1].wait_recv()
    to_sibling(2, 2)
    sibling_wait(2)
    down(0)
    up(1)
    down(1)
    v0 = stats(0)
    final(0, v0)
    v1 = stats(1)
    final(1, v1)
    for cp in oc:
        cp.wait_recv()
    for cp in started:
        cp.wait_send()


def body(
    field, w_query, w_key, w_value, w_proj, w_up, w_down, logit_scale, rel_bias, gain_attn, gain_mlp
):
    rolled = jnp.roll(field, -4, axis=2).reshape(2, 4, PART, 2, 2, 32)
    blk = rolled.transpose(3, 4, 0, 2, 1, 5).reshape(2, 2, 2, PART, 128)
    wp = jnp.stack(
        [
            jnp.concatenate([w_query, w_key, w_value, w_proj.T], axis=1),
            w_up,
            w_down.T,
        ]
    )
    flipped = rel_bias[:, ::-1, ::-1]
    table = jnp.stack([flipped[:, 7 - r:15 - r, :] for r in range(8)], axis=1)
    table = jnp.pad(table.transpose(0, 1, 3, 2), ((0, 0), (0, 0), (0, 1), (0, 0)))
    aux = jnp.concatenate(
        [
            table.reshape(3, 8, 128),
            jnp.broadcast_to(logit_scale[:, None, None], (3, 8, 128)),
            jnp.zeros((2, 8, 128), F32),
        ]
    )
    second = lax.axis_index("ch") % 2
    both = jnp.stack([gain_attn, gain_mlp])
    both = jnp.concatenate(
        [jnp.where(second == 0, both, 0.0), jnp.where(second == 1, both, 0.0)], axis=1
    )
    gain = jnp.pad(both, ((0, 6), (0, 0)))
    vmem = pl.BlockSpec(memory_space=pltpu.VMEM)
    out = pl.pallas_call(
        kernel,
        out_shape=jax.ShapeDtypeStruct((2, 2, 2, PART, 128), BF),
        in_specs=[vmem] * 4,
        out_specs=vmem,
        scratch_shapes=[
            pltpu.VMEM((3, 2, 2, NZ, 2, ROWS, PACK), BF),
            pltpu.VMEM((2, 2, PIECE, 128), BF),
            pltpu.VMEM((2, TOK, D), BF),
            pltpu.VMEM((2, 8, 32, 640), F32),
            pltpu.VMEM((8, 32, 512), F32),
            pltpu.VMEM((2, TOK, D), BF),
            pltpu.VMEM((2, 3, 64, D), BF),
            pltpu.VMEM((2, TOK, D), BF),
            pltpu.VMEM((TOK, D), BF),
            pltpu.VMEM((2, 4, PIECE, TOK), BF),
            pltpu.VMEM((2, 3, PIECE, TOK), BF),
            pltpu.VMEM((2, 8, TOK), F32),
            pltpu.VMEM((2, 3, 8, TOK), F32),
            pltpu.VMEM((2, 8, D), F32),
            pltpu.VMEM((2, 8, 8, 128), F32),
            pltpu.VMEM((2, 3, 64, 64), F32),
            pltpu.VMEM((2, 2, 2, PART, 128), BF),
            pltpu.SemaphoreType.DMA((SEMS,)),
            pltpu.SemaphoreType.DMA((SEMS,)),
        ],
        compiler_params=pltpu.CompilerParams(
            collective_id=0, has_side_effects=True, vmem_limit_bytes=52 << 20
        ),
        name="block",
    )(blk, wp, aux, gain)
    mixed = out.reshape(2, 2, 2, PART, 4, 32).transpose(2, 4, 3, 0, 1, 5)
    return jnp.roll(mixed.reshape(8, PART, 128), 4, axis=2)


def solution(mesh):
    placed = (
        P("lon", "ch", None),
        P("lon", "ch"),
        P("lon", "ch"),
        P("lon", "ch"),
        P("ch", "lon"),
        P("lon", "ch"),
        P("ch", "lon"),
        P("ch"),
        P("ch", None, None),
        P("ch"),
        P("ch"),
    )
    return jax.shard_map(
        body, mesh=mesh, in_specs=placed, out_specs=P("lon", "ch", None), check_vma=False
    )
```

time: 648 us -> 138 us (0.21)
  waiting for transfers between devices: 306 us -> 0 us
  blocking collectives: 205 us -> 0 us
  Pallas kernels: 0 us -> 129 us
  local copies, waits for them, and re-layouts: 58.6 us -> 7.74 us
  matrix products: 31.2 us -> 0 us
  other arithmetic: 19.3 us -> 0.54 us
  between operations: 15.1 us -> 0.18 us
  starting transfers between devices: 9.23 us -> 0 us
    all_gather x4 -> x0, blocking collectives: 174 us -> none  [the longest x1 47 us: body(): lax.all_gather(w_query, 'lon', axis=0, tiled=True)]
    all_gather x4 -> x0, waiting for transfers between devices: 151 us -> none  [the longest x1 79.9 us: body(): lax.all_gather(w_up, 'lon', axis=0, tiled=True)]
    reduce_scatter x2 -> x0, waiting for transfers between devices: 147 us -> none  [the longest x1 74 us: body(): lax.psum_scatter(partial_down.astype(jnp.bfloat16), 'ch', scatter_dimensi...]
    pallas_call x0 -> x1, Pallas kernels: none -> 129 us  [body(): pl.pallas_call(kernel, out_shape=jax.ShapeDtypeStruct((2, 2, 2, PART, 128...]
    dot_general x7 -> x0, matrix products: 31.2 us -> none  [the longest x1 14.9 us: body(): jnp.dot(hidden, lax.all_gather(w_down, 'lon', axis=1, tiled=True), prefer...]
    psum x2 -> x0, blocking collectives: 31.1 us -> none  [the longest x1 15.7 us: body(): lax.psum((jnp.sum(down, axis=1, keepdims=True), jnp.sum(down * down, axis...]
    gather x2 -> x0, local copies, waits for them, and re-layouts: 26.7 us -> none  [bias_and_mask(): bias = table[:, delta_row, delta_col]]
    convert_element_type x5 -> x0, local copies, waits for them, and re-layouts: 12 us -> none  [the longest x4 11.8 us: unit_rows(): array = array.astype(jnp.float32)]
  transfers between devices with their start and end apart: 8 -> 0, of which waited for: 7 -> 0; matrix products, arithmetic and copies ran while one was open for 5% -> 0% of each run, Pallas kernels for 0% -> 0%
where the time goes in v1:
time: 138 us; the launch traced here: 137 us
  Pallas kernels  129 us (93%)
  local copies, waits for them, and re-layouts  7.74 us (6%)
    pallas_call x1, Pallas kernels, body(): pl.pallas_call(kernel, out_shape=jax.ShapeDtypeStruct((2, 2, 2, PART, 128...  129 us
    unnamed x32, local copies, waits for them, and re-layouts  5.11 us

profile of v1, /device:TPU:1, one launch (start us, length us, event | category | flops | bytes accessed | tf_op | source)
XLA Modules:
  0.0 137.5 jit_solution(5003336231309354342)
XLA Ops:
  0.0 0.0 copy-start
  0.0 1.3 copy.24
  1.3 0.0 copy-done
  1.3 0.2 slice.64
  1.5 0.3 copy.23
  1.8 0.1 pad_maximum_fusion
  1.9 0.0 copy-start.4
  1.9 0.0 copy-start.5
  1.9 0.0 copy-start.6
  1.9 0.0 copy-start.7
  2.0 0.3 copy.19.blk
  2.2 0.4 copy-done.4
  2.7 0.0 copy-done.5
  2.7 0.0 copy-done.6
  2.7 0.0 copy-done.7
  2.7 0.0 copy-start.2
  2.7 0.0 copy-start.3
  2.7 0.1 maximum_bitcast_fusion
  2.8 0.8 copy-done.2
  3.6 0.0 copy-done.3
  3.6 0.0 copy-start.1
  3.7 0.7 copy-done.1
  4.4 0.1 slice.67
  4.5 0.1 slice.69
  4.5 0.1 slice.71
  4.6 0.1 slice.73
  4.7 0.1 slice.75
  4.8 0.1 slice.77
  4.9 0.1 slice.79
  5.0 0.1 slice.81
  5.1 0.2 copy.25
  5.3 0.1 reshape.18
  5.5 0.0 copy-start.10
  5.5 0.1 pad.18.clone
  5.5 0.6 copy-done.10
  6.1 0.1 pad.17.clone
  6.2 0.0 copy-start.9
  6.2 0.1 maximum_maximum_fusion.aux
  6.3 0.0 copy-start.8
  6.3 0.6 copy-done.9
  6.9 0.1 copy-done.8
  7.0 0.1 select_maximum_fusion.gain
  7.1 129.0 %block.1 = bf16[2,2,2,192,128]{4,3,2,1,0:T(8,128)(2,1)S(1)} custom-call(bf16[2,2,2,192,128]{4,3,2,1,0:T(8,128)(2,1)S(1)} %copy.19.blk, bf16[3,48,768]{2,1,0:T(8,128)(2,1)S(1)} %pad_maximum_fusion.2.wp, f32[8,8,128]{2,1,0:T(8,128)S(1)} %maximum_maximum_fusion.aux, f32[8,384]{1,0:T(8,128)S(1)} %select_maximum_fusion.gain), custom_call_target="tpu_custom_call" | custom-call | tf_op jit(solution)/shard_map/block/pallas_call | solution.py:467
  136.1 0.2 copy.20
  136.4 0.2 pad_maximum_fusion.1
  136.5 1.0 copy.22
  (16 shorter events, 0.2 us)
Async XLA Ops:
  0.0 1.3 copy-start
  1.9 0.7 copy-start.4
  1.9 0.7 copy-start.5
  1.9 0.8 copy-start.6
  1.9 0.8 copy-start.7
  2.7 0.9 copy-start.2
  2.7 0.9 copy-start.3
  3.6 0.7 copy-start.1
  5.5 0.7 copy-start.10
  6.2 0.7 copy-start.9
  6.3 0.7 copy-start.8

commit v2 on v1

v2 whole, which is shorter than its diff:
```python
import jax
import jax.numpy as jnp
from jax import lax
from jax.experimental import pallas as pl
from jax.experimental.pallas import tpu as pltpu
from jax.sharding import PartitionSpec as P

MESH = pl.DeviceIdType.MESH
BF = jnp.bfloat16
F32 = jnp.float32
D = 1536
NX, NY, NZ = 4, 4, 8
ROWS = 48
PACK = 768
TOK = 256
PART = 192
PIECE = 384
SEMS = 192


def nt(a, b):
    return lax.dot_general(a, b, (((1,), (1,)), ((), ())), preferred_element_type=F32)


def nn(a, b):
    return jnp.dot(a, b, preferred_element_type=F32)


def gelu(v):
    return 0.5 * v * (1.0 + lax.erf(v * 0.7071067811865476))


def by_column(v):
    v = v.reshape(4, 8, 8, v.shape[1])
    return jnp.concatenate([v[:, c].reshape(32, v.shape[3]) for c in range(8)], axis=0)


def kernel(
    field, w_query, w_key, w_value, w_proj, w_up, w_down, logit, rel, g_attn, g_mlp, out,
    fr, rq, rk, rv, rpj, sc, tb, rga, rgm,
    blk, gw, rin, xf, qn, kn, vn, at, pb, rl, rp, af, hs, db, rdl, rd, ss, st, ga, ea, bias, ob,
    load, send, recv,
):
    lon = lax.axis_index("lon")
    ch = lax.axis_index("ch")
    x, yl = ch // 2, ch % 2
    core, z, yh = lon % 2, (lon // 2) % NZ, lon // (2 * NZ)
    y = yh * 2 + yl
    way = 1 - 2 * core

    def at_x(dx):
        return (lon, ((x + dx + NX) % NX) * 2 + yl)

    def at_z(dz):
        return ((yh * NZ + (z + dz + NZ) % NZ) * 2 + core, ch)

    def at_y(dy):
        yy = (y + dy + NY) % NY
        return (((yy // 2) * NZ + z) * 2 + core, x * 2 + yy % 2)

    sibling = (lon + 1 - 2 * core, ch)
    partner = (lon, x * 2 + 1 - yl)

    def at_lon(dl, other):
        c = x * 2 + 1 - yl if other else ch
        return ((lon + dl + 32) % 32, c)

    def peer(dx, other):
        c = 1 - yl if other else yl
        return (lon, ((x + dx) % NX) * 2 + c)

    peers = [(1, 0), (3, 0), (2, 0), (0, 1), (1, 1), (3, 1), (2, 1)]

    loads = []
    for src, dst in (
        (field, fr), (w_query, rq), (w_key, rk), (w_value, rv), (w_proj, rpj),
        (w_up, gw.at[1, yl, yh, z, core]), (w_down, gw.at[2, yl, yh, z, core]),
        (logit, sc), (rel, tb), (g_attn, rga), (g_mlp, rgm),
    ):
        copy = pltpu.make_async_copy(src, dst, load.at[len(loads)])
        copy.start()
        loads.append(copy)

    barrier = pltpu.get_barrier_semaphore()
    greeted = [peer(a, b) for a, b in peers]
    greeted += [at_z(dz) for dz in (1, -1, 2, -2, 3, -3, 4)]
    greeted += [at_y(1), at_y(-1), at_y(2), sibling]
    greeted += [at_lon(1, 0), at_lon(1, 1), at_lon(-1, 0), at_lon(-1, 1)]
    for device in greeted:
        pl.semaphore_signal(barrier, inc=1, device_id=device, device_id_type=MESH)

    for copy in loads:
        copy.wait()

    lane = lax.broadcasted_iota(jnp.int32, (32, 128), 1) // 32

    def regroup(i, carry):
        rows = pl.ds(pl.multiple_of(i * 32, 32), 32)
        for half in range(2):
            cols = [fr[half * 4 + j, rows, :].astype(F32) for j in range(4)]
            for k in range(4):
                v = None
                for j in range(4):
                    moved = pltpu.roll(cols[j], (32 * (j - k) - 4) % 128, 1)
                    v = moved if v is None else jnp.where(lane == j, moved, v)
                blk[k // 2, k % 2, half, rows, :] = v.astype(BF)
        return carry

    lax.fori_loop(0, PART // 32, regroup, 0)
    q, k, v = (r[...].astype(F32) for r in (rq, rk, rv))
    p = rpj[...].astype(F32)
    gw[0, yl, yh, z, core] = jnp.concatenate(
        [
            q[:, :128], k[:, :128], v[:, :128], q[:, 128:], k[:, 128:],
            v[:, 128:], p[:, 128:], p[:, :128],
        ],
        axis=1,
    ).astype(BF)

    pl.semaphore_wait(barrier, len(greeted))

    started = []

    def push(src, dst, device):
        i = len(started)
        copy = pltpu.make_async_remote_copy(
            src_ref=src, dst_ref=dst, send_sem=send.at[i], recv_sem=recv.at[i],
            device_id=device, device_id_type=MESH,
        )
        copy.start()
        started.append(copy)
        return copy

    def share(ref, device):
        return push(ref, ref, device)

    UPPER, LOWER = pl.ds(0, 32), pl.ds(32, 16)
    zc, yc, yr, dc = {}, {}, {}, {}

    def wblock(t, yy, zz, rows=pl.ds(0, ROWS)):
        return gw.at[t, yy % 2, yy // 2, zz % NZ, core, rows]

    def ring_send(key, s, ref_of):
        if s < 4:
            zc[key, s, 1] = share(ref_of(z - s + 1 + NZ), at_z(1))
            zc[key, s, -1] = share(ref_of(z + s - 1), at_z(-1))
        else:
            zc[key, s, 0] = share(ref_of(z - way * 3 + NZ), at_z(way))

    def ring_wait(key, s):
        for sign in (1, -1, 0):
            if (key, s, sign) in zc:
                zc[key, s, sign].wait_recv()

    ORDER = [0, 1, -1, 2, -2, 3, -3, 4]

    def y_send_one(k):
        ref = wblock(0, y, z + ORDER[k] + NZ, UPPER)
        yc[k, 1] = share(ref, at_y(1))
        yc[k, -1] = share(ref, at_y(-1))

    def y_relay_one(k):
        yc[k, 1].wait_recv()
        yc[k, -1].wait_recv()
        sign = 1 if k % 2 == 0 else -1
        yr[k] = share(wblock(0, (y - sign + NY) % NY, z + ORDER[k] + NZ, UPPER), at_y(sign))

    def group(t, dy, zs=pl.ds(0, NZ), rows=pl.ds(0, ROWS)):
        yy = (y + dy + NY) % NY
        return gw.at[t, yy % 2, yy // 2, zs, core, rows]

    def upper(dz):
        return wblock(0, y, z + dz + NZ, UPPER)

    def lower(dz):
        return gw.at[0, :, :, (z + dz + NZ) % NZ, core, LOWER]

    def far_send(key, ref_of):
        for dz in (2, -2, 1, -1):
            zc[key, dz] = share(ref_of(0), at_z(dz))

    def far_relay(key, ref_of):
        far_wait(key, 2, -2)
        zc[key, 3] = share(ref_of(-2), at_z(1))
        zc[key, -3] = share(ref_of(2), at_z(-1))
        zc[key, 4] = share(ref_of(-2 * way), at_z(2 * way))

    def far_wait(key, *steps):
        for dz in steps:
            zc[key, dz].wait_recv()

    def y_send(*ks):
        for k in ks:
            y_send_one(k)

    def y_relay(*ks):
        for k in ks:
            y_relay_one(k)

    def lower_to_sibling(*steps):
        for dz in steps:
            to_sibling("A", lower(dz))

    HALVES = (pl.ds(0, 4), pl.ds(4, 4))

    def up_z_send(*steps):
        for dz in steps:
            zc["U", dz] = share(wblock(1, y, z), at_z(dz))

    def up_y_send():
        for dz in (1, -1, 2, -2, 3, -3, 4):
            zc["U", dz].wait_recv()
        for half in range(2):
            for sign in (1, -1):
                yc["U", half, sign] = share(group(1, 0, HALVES[half]), at_y(sign))

    def up_y_relay(half):
        yc["U", half, 1].wait_recv()
        yc["U", half, -1].wait_recv()
        sign = 1 - 2 * half
        yr["U", half] = share(group(1, -sign, HALVES[half]), at_y(sign))

    def down_y_send():
        for dy in (1, -1, 2):
            yc["D", dy] = share(wblock(2, y, z), at_y(dy))

    def down_block(part):
        return lambda zz: gw.at[2, part, :, zz % NZ, core]

    def down_z(step):
        if step == 1:
            for dy in (1, -1, 2):
                yc["D", dy].wait_recv()
        for part in range(2):
            if step > 1:
                ring_wait(("D", part), step - 1)
            if step < 5:
                ring_send(("D", part), step, down_block(part))
        here = ((0,), (1, -1), (2, -2), (3, -3), (4,))[step - 1]
        for dz in here:
            to_sibling("D", plane(2, dz))

    def to_sibling(key, ref):
        dc.setdefault(key, []).append(share(ref, sibling))

    def sibling_wait(key):
        for copy in dc[key]:
            copy.wait_recv()

    def plane(t, dz, rows=pl.ds(0, ROWS)):
        return gw.at[t, :, :, (z + dz + NZ) % NZ, core, rows]

    rows_mine = pl.ds(pl.multiple_of(yl * PART, PART), PART)
    lanes_mine = pl.ds(pl.multiple_of(x * PIECE, 128), PIECE)
    ic = {}

    def input_send(g):
        for name, src, cg, device in (
            ("partner", blk.at[1 - yl, g, 1], 0, partner),
            ("both", blk.at[1 - yl, g, 0], 1, at_lon(-1, 1)),
            ("west", blk.at[yl, g, 0], 1, at_lon(-1, 0)),
        ):
            ic[g, name] = push(src, rin.at[g, cg, rows_mine], device)

    xc, xr = {}, {}

    def x_send(g):
        rin[g, 0, rows_mine] = blk[yl, g, 1]
        for name in ("partner", "both", "west"):
            ic[g, name].wait_recv()
        for cg in range(2):
            piece = rin[g, cg].astype(F32).T.reshape(4, 4, 8, PIECE)
            for w in range(4):
                part = piece[:, w].reshape(32, PIECE).astype(BF)
                xf[g, pl.ds(w * 64 + cg * 32, 32), lanes_mine] = part
        ref = xf.at[g, :, lanes_mine]
        xc[g, 1] = share(ref, at_x(1))
        xc[g, -1] = share(ref, at_x(-1))

    def x_relay(g):
        for sign, half in ((1, 0), (-1, 1)):
            xc[g, sign].wait_recv()
            lanes = pl.ds(pl.multiple_of(((x + 4 - sign) % NX) * PIECE, 128), PIECE)
            xr[g, sign] = share(xf.at[g, pl.ds(half * 128, 128), lanes], at_x(sign))

    def tables():
        k_of = lax.broadcasted_iota(jnp.int32, (15, 128), 1) // 8
        a_of = (
            lax.broadcasted_iota(jnp.int32, (8, 128), 1) % 8
            - lax.broadcasted_iota(jnp.int32, (8, 128), 0)
            + 7
        )
        for h in range(3):
            t = tb[h]
            wide = jnp.zeros((15, 128), F32)
            for b in range(15):
                wide = jnp.where(k_of == b, t[:, b:b + 1], wide)
            e = jnp.zeros((8, 128), F32)
            for a in range(15):
                e = jnp.where(a_of == a, wide[a:a + 1, :], e)
            ea[yl, h] = e
            ea[yl, 3 + h] = jnp.broadcast_to(sc[0:1, h:h + 1], (8, 128))
        copies = [share(ea.at[yl], partner)]
        here = lax.broadcasted_iota(jnp.int32, (1, PIECE), 1) // PART == yl
        rows = [
            jnp.where(here, jnp.concatenate([r[...], r[...]], axis=1), 0.0) for r in (rga, rgm)
        ]
        ga[yl, :, lanes_mine] = jnp.concatenate(rows + [jnp.zeros((6, PIECE), F32)], axis=0)
        ref = ga.at[yl, :, lanes_mine]
        return copies + [share(ref, peer(a, b)) for a, b in peers]

    row_j = lax.broadcasted_iota(jnp.int32, (64, 128), 0) % 8
    row_i = lax.broadcasted_iota(jnp.int32, (64, 128), 1) % 8
    poles = jnp.where((row_i >= 4) != (row_j >= 4), -1e9, 0.0).astype(F32)
    low = lax.broadcasted_iota(jnp.int32, (64, 128), 1) < 64
    low_bf = jnp.where(low, 1.0, 0.0).astype(BF)
    high_bf = jnp.where(low, 0.0, 1.0).astype(BF)
    HEADS_OF = [((0, 0), (0, 1)), ((1, 0), (1, 1)), ((0, 2), (1, 2))]

    def biases():
        for pair, members in enumerate(HEADS_OF):
            t0, t1 = (ea[part, h] for part, h in members)
            for cj in range(8):
                lo = (7 - cj) * 8
                bias[pair, pl.ds(cj * 8, 8), :] = jnp.concatenate(
                    [t0[:, lo:lo + 64], t1[:, lo:lo + 64]], axis=1
                )

    def unit(v):
        n = v.shape[1]
        same = (
            lax.broadcasted_iota(jnp.int32, (n, n), 0) // 64
            == lax.broadcasted_iota(jnp.int32, (n, n), 1) // 64
        )
        ones = jnp.where(same, 1.0, 0.0).astype(BF)
        square = v * v
        head = square.astype(BF)
        rest = (square - head.astype(F32)).astype(BF)
        total = nn(head, ones) + nn(rest, ones)
        return v * lax.rsqrt(total + 1e-6)

    def qkv(g):
        xr[g, 1].wait_recv()
        xr[g, -1].wait_recv()
        thirds = []
        for part in range(2):

            def product(lo, size):
                w = gw[0, part, :, :, :, :, lo:lo + size].reshape(D, size)
                return nn(xf[g], w).astype(BF).astype(F32)

            r = unit(product(0, 256))
            qn[part] = r[:, :128].astype(BF)
            kn[part] = r[:, 128:].astype(BF)
            r = product(256, 256)
            vn[part] = r[:, :128].astype(BF)
            thirds.append((unit(r[:, 128:]), product(512, 128)))
        first = lax.broadcasted_iota(jnp.int32, (TOK, 128), 1) < 64
        (a0, v0), (a1, v1) = thirds
        qn[2] = jnp.where(first, a0, pltpu.roll(a1, 64, 1)).astype(BF)
        kn[2] = jnp.where(first, pltpu.roll(a0, 64, 1), a1).astype(BF)
        vn[2] = jnp.where(first, v0, pltpu.roll(v1, 64, 1)).astype(BF)

    def windows(g):
        def window(w, carry):
            rows = pl.ds(pl.multiple_of(w * 64, 64), 64)
            for pair, ((p0, h0), (p1, h1)) in enumerate(HEADS_OF):
                qq = qn[pair, rows]
                both = jnp.concatenate([qq * low_bf, qq * high_bf], axis=0)
                s = nt(kn[pair, rows], both)
                scale = jnp.where(low[0:1], ea[p0, 3 + h0, 0:1, :], ea[p1, 3 + h1, 0:1, :])
                s = s * scale + bias[pair]
                if g == 1:
                    s = s + jnp.where(jnp.logical_and(yl == 1, w == 3), poles, 0.0)
                e = jnp.exp(s - jnp.max(s, axis=0, keepdims=True))
                e = e * (1.0 / jnp.sum(e, axis=0, keepdims=True))
                o = nn(e.T.astype(BF), vn[pair, rows])
                o = jnp.where(low, o[:64], o[64:])
                if pair < 2:
                    at[pair, rows, 128:256] = o.astype(BF)
                else:
                    at[0, rows, 0:128] = jnp.where(low, 0.0, pltpu.roll(o, 64, 1)).astype(BF)
                    at[1, rows, 0:128] = jnp.where(low, 0.0, o).astype(BF)
            return carry

        for w in range(4):
            window(w, 0)

    def x_rows(dx):
        return pl.ds(pl.multiple_of(((x + dx + NX) % NX) * 64, 64), 64)

    LEFT, RIGHT = pl.ds(0, 768), pl.ds(768, 768)
    pc = {}

    def proj(g):
        def columns(n, carry):
            total = None
            for part in range(2):
                w = gw[0, part, n // 2, pl.ds((n % 2) * 4, 4), :, :, 512:768].reshape(PIECE, 256)
                term = nt(at[part], w)
                total = term if total is None else total + term
            pb[g, :, pl.ds(pl.multiple_of(n * PIECE, 128), PIECE)] = total.astype(BF)
            return carry

        lax.fori_loop(0, 4, columns, 0)
        pc[g, "l", 1] = push(pb.at[g, x_rows(2), LEFT], rl.at[g, 0], at_x(1))
        pc[g, "l", -1] = push(pb.at[g, x_rows(2), RIGHT], rl.at[g, 1], at_x(-1))
        pc[g, "n", 1] = push(pb.at[g, x_rows(1), RIGHT], rp.at[g, 0, :, RIGHT], at_x(1))
        pc[g, "n", -1] = push(pb.at[g, x_rows(-1), LEFT], rp.at[g, 1, :, LEFT], at_x(-1))

    def proj_relay(g):
        for slot, (sign, lanes) in enumerate(((1, LEFT), (-1, RIGHT))):
            pc[g, "l", sign].wait_recv()
            rows = x_rows(sign)
            v = pb[g, rows, lanes].astype(F32) + rl[g, slot].astype(F32)
            pb[g, rows, lanes] = v.astype(BF)
            pc[g, "s", sign] = push(pb.at[g, rows, lanes], rp.at[g, slot, :, lanes], at_x(sign))

    ac, ar = {}, {}

    def norm_one(g):
        for what in ("n", "s"):
            for sign in (1, -1):
                pc[g, what, sign].wait_recv()
        v = pb[g, x_rows(0), :].astype(F32) + rp[g, 0].astype(F32) + rp[g, 1].astype(F32)
        mean = jnp.sum(v, axis=1, keepdims=True) * (1.0 / D)
        var = jnp.sum(v * v, axis=1, keepdims=True) * (1.0 / D) - mean * mean
        gains = ga[0, 0:1, :] + ga[1, 0:1, :]
        res = xf[g, x_rows(0), :].astype(F32)
        af[g, x_rows(0), :] = (res + (v - mean) * lax.rsqrt(var + 1e-5) * gains).astype(BF)
        ref = af.at[g, x_rows(0)]
        ac[g, 1] = share(ref, at_x(1))
        ac[g, -1] = share(ref, at_x(-1))

    def a_relay(g):
        for sign, half in ((1, 0), (-1, 1)):
            ac[g, sign].wait_recv()
            start = ((x + 4 - sign) % NX) * 64 + half * 32
            ref = af.at[g, pl.ds(pl.multiple_of(start, 32), 32)]
            ar[g, sign] = share(ref, at_x(sign))

    def up(g):
        ar[g, 1].wait_recv()
        ar[g, -1].wait_recv()

        def columns(n, carry):
            lo = pl.multiple_of((n % 3) * 256, 256)
            w = gw[1, n // 3, :, :, :, :, pl.ds(lo, 256)].reshape(D, 256)
            v = by_column(gelu(nn(af[g], w))).astype(BF)
            hs[:, pl.ds(pl.multiple_of(n * 256, 256), 256)] = v
            return carry

        lax.fori_loop(0, 6, columns, 0)

    TOP, BOTTOM = pl.ds(0, PART), pl.ds(PART, PART)
    rc = {}

    def down(g):
        for slot, dx in ((0, 2), (1, 1), (2, 3), (3, 0)):
            xx = (x + dx) % NX
            total = None
            for part in range(2):
                w = gw[2, part, xx // 2, pl.ds((xx % 2) * 4, 4)].reshape(PIECE, PACK)
                term = nt(w, hs[:, part * PACK:part * PACK + PACK])
                total = term if total is None else total + term
            db[g, slot] = total.astype(BF)
            if slot == 0:
                rc[g, "l", 1] = push(db.at[g, 0, TOP], rdl.at[g, 0], at_x(1))
                rc[g, "l", -1] = push(db.at[g, 0, BOTTOM], rdl.at[g, 1], at_x(-1))
            elif slot == 1:
                rc[g, "n", 1] = push(db.at[g, 1, BOTTOM], rd.at[g, 0, BOTTOM], at_x(1))
            elif slot == 2:
                rc[g, "n", -1] = push(db.at[g, 2, TOP], rd.at[g, 1, TOP], at_x(-1))

    def down_relay(g):
        for slot, (sign, rows) in enumerate(((1, TOP), (-1, BOTTOM))):
            rc[g, "l", sign].wait_recv()
            v = db[g, slot + 1, rows].astype(F32) + rdl[g, slot].astype(F32)
            db[g, slot + 1, rows] = v.astype(BF)
            rc[g, "s", sign] = push(db.at[g, slot + 1, rows], rd.at[g, slot, rows], at_x(sign))

    tc = {}

    def stats(g):
        for what in ("n", "s"):
            for sign in (1, -1):
                rc[g, what, sign].wait_recv()
        v = db[g, 3].astype(F32) + rd[g, 0].astype(F32) + rd[g, 1].astype(F32)
        ss[g, 0:1, :] = jnp.sum(v, axis=0, keepdims=True)
        ss[g, 1:2, :] = jnp.sum(v * v, axis=0, keepdims=True)
        for slot, dx in ((0, 2), (1, 1), (2, 3)):
            tc[g, slot] = push(ss.at[g], st.at[g, slot], at_x(dx))
        return v

    oc = []

    def final(g, v):
        res = by_column(af[g, :, lanes_mine].astype(F32)).T
        row = ga[0, 1:2, lanes_mine] + ga[1, 1:2, lanes_mine]
        col = jnp.broadcast_to(row, (128, PIECE)).T
        gains = jnp.concatenate([col, col], axis=1)
        for slot in range(3):
            tc[g, slot].wait_recv()
        tot = ss[g] + st[g, 0] + st[g, 1] + st[g, 2]
        mean = tot[0:1] * (1.0 / D)
        var = tot[1:2] * (1.0 / D) - mean * mean
        o = (res + (v - mean) * lax.rsqrt(var + 1e-5) * gains).astype(BF)
        for cg in range(2):
            ob[g, cg] = o[:, cg * 128:cg * 128 + 128].reshape(2, PART, 128)
        out[yl, g, 1] = ob[g, 0, yl]
        for src, half, device in (
            (ob.at[g, 0, 1 - yl], 1, partner),
            (ob.at[g, 1, 1 - yl], 0, at_lon(1, 1)),
            (ob.at[g, 1, yl], 0, at_lon(1, 0)),
        ):
            oc.append(push(src, out.at[yl, g, half], device))

    input_send(0)
    far_send("upper", upper)
    for dy in (1, -1, 2):
        yc["first", dy] = share(wblock(0, y, z, LOWER), at_y(dy))
    y_send(0)
    ss[...] = jnp.zeros_like(ss)
    far_relay("upper", upper)
    for dy in (1, -1, 2):
        yc["first", dy].wait_recv()
    far_send("lower", lower)
    far_wait("upper", 1, -1)
    y_send(1, 2, 3, 4)
    lower_to_sibling(0)
    input_send(1)
    x_send(0)
    far_relay("lower", lower)
    lower_to_sibling(2, -2)
    far_wait("upper", 3, -3)
    y_send(5, 6)
    y_relay(0)
    far_wait("upper", 4)
    y_send(7)
    to_sibling("A", group(0, 0, rows=UPPER))
    x_relay(0)
    y_relay(1, 2, 3, 4)
    x_send(1)
    small = tables()
    far_wait("lower", 1, -1)
    lower_to_sibling(1, -1)
    y_relay(5, 6, 7)
    up_z_send(2, -2, 3, -3, 1, -1, 4)
    down_y_send()
    to_sibling("A", group(0, 1, rows=UPPER))
    to_sibling("A", group(0, -1, rows=UPPER))
    x_relay(1)
    far_wait("lower", 3, -3, 4)
    lower_to_sibling(3, -3, 4)
    for copy in small:
        copy.wait_recv()
    biases()
    for k in range(8):
        yr[k].wait_recv()
    to_sibling("A", group(0, 2, rows=UPPER))
    sibling_wait("A")
    qkv(0)
    down_z(1)
    windows(0)
    proj(0)
    up_y_send()
    to_sibling("U", group(1, 0))
    qkv(1)
    down_z(2)
    windows(1)
    proj_relay(0)
    proj(1)
    up_y_relay(0)
    norm_one(0)
    down_z(3)
    proj_relay(1)
    up_y_relay(1)
    to_sibling("U", group(1, 1))
    to_sibling("U", group(1, -1))
    a_relay(0)
    down_z(4)
    norm_one(1)
    yr["U", 0].wait_recv()
    yr["U", 1].wait_recv()
    to_sibling("U", group(1, 2))
    sibling_wait("U")
    up(0)
    a_relay(1)
    down_z(5)
    sibling_wait("D")
    down(0)
    up(1)
    down_relay(0)
    down(1)
    v0 = stats(0)
    down_relay(1)
    final(0, v0)
    v1 = stats(1)
    final(1, v1)
    for cp in oc:
        cp.wait_recv()
    for cp in started:
        cp.wait_send()


def body(
    field, w_query, w_key, w_value, w_proj, w_up, w_down, logit_scale, rel_bias, gain_attn, gain_mlp
):
    anywhere = pl.BlockSpec(memory_space=pl.ANY)
    out = pl.pallas_call(
        kernel,
        out_shape=jax.ShapeDtypeStruct((2, 2, 2, PART, 128), BF),
        in_specs=[anywhere] * 11,
        out_specs=pl.BlockSpec(memory_space=pltpu.VMEM),
        scratch_shapes=[
            pltpu.VMEM((8, PART, 128), BF),
            pltpu.VMEM((ROWS, PART), BF),
            pltpu.VMEM((ROWS, PART), BF),
            pltpu.VMEM((ROWS, PART), BF),
            pltpu.VMEM((ROWS, PART), BF),
            pltpu.VMEM((1, 3), F32),
            pltpu.VMEM((3, 15, 15), F32),
            pltpu.VMEM((1, PART), F32),
            pltpu.VMEM((1, PART), F32),
            pltpu.VMEM((2, 2, 2, PART, 128), BF),
            pltpu.VMEM((3, 2, 2, NZ, 2, ROWS, PACK), BF),
            pltpu.VMEM((2, 2, PIECE, 128), BF),
            pltpu.VMEM((2, TOK, D), BF),
            pltpu.VMEM((3, TOK, 128), BF),
            pltpu.VMEM((3, TOK, 128), BF),
            pltpu.VMEM((3, TOK, 128), BF),
            pltpu.VMEM((2, TOK, 256), BF),
            pltpu.VMEM((2, TOK, D), BF),
            pltpu.VMEM((2, 2, 64, 768), BF),
            pltpu.VMEM((2, 2, 64, D), BF),
            pltpu.VMEM((2, TOK, D), BF),
            pltpu.VMEM((TOK, D), BF),
            pltpu.VMEM((2, 4, PIECE, TOK), BF),
            pltpu.VMEM((2, 2, PART, TOK), BF),
            pltpu.VMEM((2, 2, PIECE, TOK), BF),
            pltpu.VMEM((2, 8, TOK), F32),
            pltpu.VMEM((2, 3, 8, TOK), F32),
            pltpu.VMEM((2, 8, D), F32),
            pltpu.VMEM((2, 8, 8, 128), F32),
            pltpu.VMEM((3, 64, 128), F32),
            pltpu.VMEM((2, 2, 2, PART, 128), BF),
            pltpu.SemaphoreType.DMA((11,)),
            pltpu.SemaphoreType.DMA((SEMS,)),
            pltpu.SemaphoreType.DMA((SEMS,)),
        ],
        compiler_params=pltpu.CompilerParams(
            collective_id=0, has_side_effects=True, vmem_limit_bytes=60 << 20
        ),
        name="block",
    )(
        field, w_query, w_key, w_value, w_proj.T, w_up, w_down.T,
        logit_scale.reshape(1, 3), rel_bias, gain_attn.reshape(1, PART), gain_mlp.reshape(1, PART),
    )
    mixed = out.reshape(2, 2, 2, PART, 4, 32).transpose(2, 4, 3, 0, 1, 5)
    return jnp.roll(mixed.reshape(8, PART, 128), 4, axis=2)


def solution(mesh):
    placed = (
        P("lon", "ch", None),
        P("lon", "ch"),
        P("lon", "ch"),
        P("lon", "ch"),
        P("ch", "lon"),
        P("lon", "ch"),
        P("ch", "lon"),
        P("ch"),
        P("ch", None, None),
        P("ch"),
        P("ch"),
    )
    return jax.shard_map(
        body, mesh=mesh, in_specs=placed, out_specs=P("lon", "ch", None), check_vma=False
    )
```

time: 138 us -> 109 us (0.79)
  Pallas kernels: 129 us -> 107 us
  local copies, waits for them, and re-layouts: 7.74 us -> 2.2 us
    pallas_call x1, Pallas kernels: 129 us -> 107 us  [body(): pl.pallas_call(kernel, out_shape=jax.ShapeDtypeStruct((2, 2, 2, PART, 128...]
    unnamed x32 -> x0, local copies, waits for them, and re-layouts: 5.11 us -> none
where the time goes in v2:
time: 109 us
  Pallas kernels  107 us (98%)
  local copies, waits for them, and re-layouts  2.2 us (2%)
    pallas_call x1, Pallas kernels, body(): pl.pallas_call(kernel, out_shape=jax.ShapeDtypeStruct((2, 2, 2, PART, 128...  107 us

profile of v2, /device:TPU:1, one launch (start us, length us, event | category | flops | bytes accessed | tf_op | source)
XLA Modules:
  0.0 109.2 jit_solution(3058425023703092618)
XLA Ops:
  0.0 106.9 %block.1 = bf16[2,2,2,192,128]{4,3,2,1,0:T(8,128)(2,1)} custom-call(bf16[8,192,128]{2,1,0:T(8,128)(2,1)} %field.1, bf16[48,192]{1,0:T(8,128)(2,1)} %w_query.1, bf16[48,192]{1,0:T(8,128)(2,1)} %w_key.1, bf16[48,192]{1,0:T(8,128)(2,1)} %w_value.1, bf16[48,192]{1,0:T(8,128)(2,1)} %bitcast.14, bf16[48,768]{1,0:T(8,128)(2,1)} %w_up.1, bf16[48,768]{1,0:T(8,128)(2,1)} %bitcast.13, ...), custom_call_target="tpu_custom_call" | custom-call | tf_op jit(solution)/shard_map/block/pallas_call | solution.py:610
  106.9 1.2 %copy.13 = bf16[2,2,2,192,128]{3,4,2,1,0:T(8,128)(2,1)S(1)} copy(bf16[2,2,2,192,128]{4,3,2,1,0:T(8,128)(2,1)} %block.1) | data formatting | bytes 786432 | tf_op jit(solution)/shard_map/block/pallas_call | solution.py:610
  108.1 0.2 pad_maximum_fusion
  108.3 1.0 copy.15
  (2 shorter events, 0.1 us)

commit v3 on v2

--- a/solution.py
+++ b/solution.py
@@ -15,7 +15,7 @@
 TOK = 256
 PART = 192
 PIECE = 384
-SEMS = 192
+SEMS = 224
 
 
 def nt(a, b):
@@ -38,7 +38,7 @@
 def kernel(
     field, w_query, w_key, w_value, w_proj, w_up, w_down, logit, rel, g_attn, g_mlp, out,
     fr, rq, rk, rv, rpj, sc, tb, rga, rgm,
-    blk, gw, rin, xf, qn, kn, vn, at, pb, rl, rp, af, hs, db, rdl, rd, ss, st, ga, ea, bias, ob,
+    blk, gw, rin, xf, qn, kn, vn, third, at, pb, rl, rp, af, hs, db, rdl, rd, ss, st, ga, ea, bias, ob,
     load, send, recv,
 ):
     lon = lax.axis_index("lon")
@@ -172,11 +172,11 @@
     def upper(dz):
         return wblock(0, y, z + dz + NZ, UPPER)
 
-    def lower(dz):
-        return gw.at[0, :, :, (z + dz + NZ) % NZ, core, LOWER]
-
-    def far_send(key, ref_of):
-        for dz in (2, -2, 1, -1):
+    def lower(part):
+        return lambda dz: gw.at[0, part, :, (z + dz + NZ) % NZ, core, LOWER]
+
+    def far_send(key, ref_of, steps=(2, -2, 1, -1)):
+        for dz in steps:
             zc[key, dz] = share(ref_of(0), at_z(dz))
 
     def far_relay(key, ref_of):
@@ -199,17 +199,24 @@
 
     def lower_to_sibling(*steps):
         for dz in steps:
-            to_sibling("A", lower(dz))
+            to_sibling("A", gw.at[0, :, :, (z + dz + NZ) % NZ, core, LOWER])
+
+    def lower_send():
+        for steps in ((2, -2), (1, -1)):
+            for part in range(2):
+                far_send(("lower", part), lower(part), steps)
+
+    def lower_wait(*steps):
+        for part in range(2):
+            far_wait(("lower", part), *steps)
 
     HALVES = (pl.ds(0, 4), pl.ds(4, 4))
 
-    def up_z_send(*steps):
-        for dz in steps:
-            zc["U", dz] = share(wblock(1, y, z), at_z(dz))
+    def up_block(dz):
+        return wblock(1, y, z + dz + NZ)
 
     def up_y_send():
-        for dz in (1, -1, 2, -2, 3, -3, 4):
-            zc["U", dz].wait_recv()
+        far_wait("U", 1, -1, 3, -3, 4)
         for half in range(2):
             for sign in (1, -1):
                 yc["U", half, sign] = share(group(1, 0, HALVES[half]), at_y(sign))
@@ -273,13 +280,14 @@
             for w in range(4):
                 part = piece[:, w].reshape(32, PIECE).astype(BF)
                 xf[g, pl.ds(w * 64 + cg * 32, 32), lanes_mine] = part
-        ref = xf.at[g, :, lanes_mine]
-        xc[g, 1] = share(ref, at_x(1))
-        xc[g, -1] = share(ref, at_x(-1))
+        for half in range(2):
+            for sign in (1, -1):
+                rows = pl.ds((half if sign == 1 else 1 - half) * 128, 128)
+                xc[g, sign, half] = share(xf.at[g, rows, lanes_mine], at_x(sign))
 
     def x_relay(g):
         for sign, half in ((1, 0), (-1, 1)):
-            xc[g, sign].wait_recv()
+            xc[g, sign, 0].wait_recv()
             lanes = pl.ds(pl.multiple_of(((x + 4 - sign) % NX) * PIECE, 128), PIECE)
             xr[g, sign] = share(xf.at[g, pl.ds(half * 128, 128), lanes], at_x(sign))
 
@@ -339,42 +347,45 @@
         total = nn(head, ones) + nn(rest, ones)
         return v * lax.rsqrt(total + 1e-6)
 
-    def qkv(g):
-        xr[g, 1].wait_recv()
-        xr[g, -1].wait_recv()
-        thirds = []
-        for part in range(2):
-
-            def product(lo, size):
-                w = gw[0, part, :, :, :, :, lo:lo + size].reshape(D, size)
-                return nn(xf[g], w).astype(BF).astype(F32)
-
-            r = unit(product(0, 256))
-            qn[part] = r[:, :128].astype(BF)
-            kn[part] = r[:, 128:].astype(BF)
-            r = product(256, 256)
-            vn[part] = r[:, :128].astype(BF)
-            thirds.append((unit(r[:, 128:]), product(512, 128)))
+    def whole(g):
+        for sign in (1, -1):
+            xc[g, sign, 1].wait_recv()
+            xr[g, sign].wait_recv()
+
+    def qkv(g, part):
+        def product(lo, size):
+            w = gw[0, part, :, :, :, :, lo:lo + size].reshape(D, size)
+            return nn(xf[g], w).astype(BF).astype(F32)
+
+        r = unit(product(0, 256))
+        qn[g, part] = r[:, :128].astype(BF)
+        kn[g, part] = r[:, 128:].astype(BF)
+        r = product(256, 256)
+        vn[g, part] = r[:, :128].astype(BF)
+        third[g, part, 0] = unit(r[:, 128:])
+        third[g, part, 1] = product(512, 128)
+
+    def third_pair(g):
         first = lax.broadcasted_iota(jnp.int32, (TOK, 128), 1) < 64
-        (a0, v0), (a1, v1) = thirds
-        qn[2] = jnp.where(first, a0, pltpu.roll(a1, 64, 1)).astype(BF)
-        kn[2] = jnp.where(first, pltpu.roll(a0, 64, 1), a1).astype(BF)
-        vn[2] = jnp.where(first, v0, pltpu.roll(v1, 64, 1)).astype(BF)
+        (a0, v0), (a1, v1) = ((third[g, part, 0], third[g, part, 1]) for part in range(2))
+        qn[g, 2] = jnp.where(first, a0, pltpu.roll(a1, 64, 1)).astype(BF)
+        kn[g, 2] = jnp.where(first, pltpu.roll(a0, 64, 1), a1).astype(BF)
+        vn[g, 2] = jnp.where(first, v0, pltpu.roll(v1, 64, 1)).astype(BF)
 
     def windows(g):
         def window(w, carry):
             rows = pl.ds(pl.multiple_of(w * 64, 64), 64)
             for pair, ((p0, h0), (p1, h1)) in enumerate(HEADS_OF):
-                qq = qn[pair, rows]
+                qq = qn[g, pair, rows]
                 both = jnp.concatenate([qq * low_bf, qq * high_bf], axis=0)
-                s = nt(kn[pair, rows], both)
+                s = nt(kn[g, pair, rows], both)
                 scale = jnp.where(low[0:1], ea[p0, 3 + h0, 0:1, :], ea[p1, 3 + h1, 0:1, :])
                 s = s * scale + bias[pair]
                 if g == 1:
                     s = s + jnp.where(jnp.logical_and(yl == 1, w == 3), poles, 0.0)
                 e = jnp.exp(s - jnp.max(s, axis=0, keepdims=True))
                 e = e * (1.0 / jnp.sum(e, axis=0, keepdims=True))
-                o = nn(e.T.astype(BF), vn[pair, rows])
+                o = nn(e.T.astype(BF), vn[g, pair, rows])
                 o = jnp.where(low, o[:64], o[64:])
                 if pair < 2:
                     at[pair, rows, 128:256] = o.astype(BF)
@@ -428,20 +439,23 @@
         gains = ga[0, 0:1, :] + ga[1, 0:1, :]
         res = xf[g, x_rows(0), :].astype(F32)
         af[g, x_rows(0), :] = (res + (v - mean) * lax.rsqrt(var + 1e-5) * gains).astype(BF)
-        ref = af.at[g, x_rows(0)]
-        ac[g, 1] = share(ref, at_x(1))
-        ac[g, -1] = share(ref, at_x(-1))
+        for half in range(2):
+            for sign in (1, -1):
+                start = x * 64 + (half if sign == 1 else 1 - half) * 32
+                ref = af.at[g, pl.ds(pl.multiple_of(start, 32), 32)]
+                ac[g, sign, half] = share(ref, at_x(sign))
 
     def a_relay(g):
         for sign, half in ((1, 0), (-1, 1)):
-            ac[g, sign].wait_recv()
+            ac[g, sign, 0].wait_recv()
             start = ((x + 4 - sign) % NX) * 64 + half * 32
             ref = af.at[g, pl.ds(pl.multiple_of(start, 32), 32)]
             ar[g, sign] = share(ref, at_x(sign))
 
     def up(g):
-        ar[g, 1].wait_recv()
-        ar[g, -1].wait_recv()
+        for sign in (1, -1):
+            ac[g, sign, 1].wait_recv()
+            ar[g, sign].wait_recv()
 
         def columns(n, carry):
             lo = pl.multiple_of((n % 3) * 256, 256)
@@ -454,6 +468,9 @@
 
     TOP, BOTTOM = pl.ds(0, PART), pl.ds(PART, PART)
     rc = {}
+
+    def half(c):
+        return pl.ds(c * 128, 128)
 
     def down(g):
         for slot, dx in ((0, 2), (1, 1), (2, 3), (3, 0)):
@@ -464,108 +481,126 @@
                 term = nt(w, hs[:, part * PACK:part * PACK + PACK])
                 total = term if total is None else total + term
             db[g, slot] = total.astype(BF)
-            if slot == 0:
-                rc[g, "l", 1] = push(db.at[g, 0, TOP], rdl.at[g, 0], at_x(1))
-                rc[g, "l", -1] = push(db.at[g, 0, BOTTOM], rdl.at[g, 1], at_x(-1))
-            elif slot == 1:
-                rc[g, "n", 1] = push(db.at[g, 1, BOTTOM], rd.at[g, 0, BOTTOM], at_x(1))
-            elif slot == 2:
-                rc[g, "n", -1] = push(db.at[g, 2, TOP], rd.at[g, 1, TOP], at_x(-1))
-
-    def down_relay(g):
+            for c in range(2):
+                if slot == 0:
+                    for to, (sign, rows) in enumerate(((1, TOP), (-1, BOTTOM))):
+                        rc[g, c, "l", sign] = push(
+                            db.at[g, 0, rows, half(c)], rdl.at[g, to, :, half(c)], at_x(sign)
+                        )
+                elif slot < 3:
+                    sign, rows = ((1, BOTTOM), (-1, TOP))[slot - 1]
+                    rc[g, c, "n", sign] = push(
+                        db.at[g, slot, rows, half(c)],
+                        rd.at[g, slot - 1, rows, half(c)],
+                        at_x(sign),
+                    )
+
+    def down_relay(g, c):
         for slot, (sign, rows) in enumerate(((1, TOP), (-1, BOTTOM))):
-            rc[g, "l", sign].wait_recv()
-            v = db[g, slot + 1, rows].astype(F32) + rdl[g, slot].astype(F32)
-            db[g, slot + 1, rows] = v.astype(BF)
-            rc[g, "s", sign] = push(db.at[g, slot + 1, rows], rd.at[g, slot, rows], at_x(sign))
+            rc[g, c, "l", sign].wait_recv()
+            v = db[g, slot + 1, rows, half(c)].astype(F32)
+            v = v + rdl[g, slot, :, half(c)].astype(F32)
+            db[g, slot + 1, rows, half(c)] = v.astype(BF)
+            rc[g, c, "s", sign] = push(
+                db.at[g, slot + 1, rows, half(c)], rd.at[g, slot, rows, half(c)], at_x(sign)
+            )
 
     tc = {}
 
-    def stats(g):
+    def stats(g, c):
         for what in ("n", "s"):
             for sign in (1, -1):
-                rc[g, what, sign].wait_recv()
-        v = db[g, 3].astype(F32) + rd[g, 0].astype(F32) + rd[g, 1].astype(F32)
-        ss[g, 0:1, :] = jnp.sum(v, axis=0, keepdims=True)
-        ss[g, 1:2, :] = jnp.sum(v * v, axis=0, keepdims=True)
+                rc[g, c, what, sign].wait_recv()
+        v = db[g, 3, :, half(c)].astype(F32)
+        v = v + rd[g, 0, :, half(c)].astype(F32) + rd[g, 1, :, half(c)].astype(F32)
+        ss[g, c, 0:1, :] = jnp.sum(v, axis=0, keepdims=True)
+        ss[g, c, 1:2, :] = jnp.sum(v * v, axis=0, keepdims=True)
         for slot, dx in ((0, 2), (1, 1), (2, 3)):
-            tc[g, slot] = push(ss.at[g], st.at[g, slot], at_x(dx))
+            tc[g, c, slot] = push(ss.at[g, c], st.at[g, c, slot], at_x(dx))
         return v
 
     oc = []
 
-    def final(g, v):
+    def residual(g):
         res = by_column(af[g, :, lanes_mine].astype(F32)).T
         row = ga[0, 1:2, lanes_mine] + ga[1, 1:2, lanes_mine]
-        col = jnp.broadcast_to(row, (128, PIECE)).T
-        gains = jnp.concatenate([col, col], axis=1)
+        return res, jnp.broadcast_to(row, (128, PIECE)).T
+
+    def final(g, c, v, res, gains):
         for slot in range(3):
-            tc[g, slot].wait_recv()
-        tot = ss[g] + st[g, 0] + st[g, 1] + st[g, 2]
+            tc[g, c, slot].wait_recv()
+        tot = ss[g, c] + st[g, c, 0] + st[g, c, 1] + st[g, c, 2]
         mean = tot[0:1] * (1.0 / D)
         var = tot[1:2] * (1.0 / D) - mean * mean
-        o = (res + (v - mean) * lax.rsqrt(var + 1e-5) * gains).astype(BF)
-        for cg in range(2):
-            ob[g, cg] = o[:, cg * 128:cg * 128 + 128].reshape(2, PART, 128)
-        out[yl, g, 1] = ob[g, 0, yl]
-        for src, half, device in (
-            (ob.at[g, 0, 1 - yl], 1, partner),
-            (ob.at[g, 1, 1 - yl], 0, at_lon(1, 1)),
-            (ob.at[g, 1, yl], 0, at_lon(1, 0)),
-        ):
-            oc.append(push(src, out.at[yl, g, half], device))
-
-    input_send(0)
+        o = res[:, c * 128:c * 128 + 128] + (v - mean) * lax.rsqrt(var + 1e-5) * gains
+        ob[g, c] = o.astype(BF).reshape(2, PART, 128)
+        if c == 0:
+            out[yl, g, 1] = ob[g, 0, yl]
+            oc.append(push(ob.at[g, 0, 1 - yl], out.at[yl, g, 1], partner))
+        else:
+            oc.append(push(ob.at[g, 1, 1 - yl], out.at[yl, g, 0], at_lon(1, 1)))
+            oc.append(push(ob.at[g, 1, yl], out.at[yl, g, 0], at_lon(1, 0)))
+
     far_send("upper", upper)
     for dy in (1, -1, 2):
         yc["first", dy] = share(wblock(0, y, z, LOWER), at_y(dy))
+    input_send(0)
     y_send(0)
+    small = tables()
     ss[...] = jnp.zeros_like(ss)
     far_relay("upper", upper)
     for dy in (1, -1, 2):
         yc["first", dy].wait_recv()
-    far_send("lower", lower)
+    lower_send()
+    input_send(1)
     far_wait("upper", 1, -1)
     y_send(1, 2, 3, 4)
     lower_to_sibling(0)
-    input_send(1)
     x_send(0)
-    far_relay("lower", lower)
-    lower_to_sibling(2, -2)
     far_wait("upper", 3, -3)
     y_send(5, 6)
-    y_relay(0)
     far_wait("upper", 4)
     y_send(7)
+    y_relay(0)
+    far_relay(("lower", 0), lower(0))
+    far_relay(("lower", 1), lower(1))
+    far_send("U", up_block)
+    lower_to_sibling(2, -2)
     to_sibling("A", group(0, 0, rows=UPPER))
     x_relay(0)
     y_relay(1, 2, 3, 4)
     x_send(1)
-    small = tables()
-    far_wait("lower", 1, -1)
+    lower_wait(1, -1)
     lower_to_sibling(1, -1)
     y_relay(5, 6, 7)
-    up_z_send(2, -2, 3, -3, 1, -1, 4)
     down_y_send()
     to_sibling("A", group(0, 1, rows=UPPER))
     to_sibling("A", group(0, -1, rows=UPPER))
+    lower_wait(3, -3, 4)
+    lower_to_sibling(3, -3, 4)
     x_relay(1)
-    far_wait("lower", 3, -3, 4)
-    lower_to_sibling(3, -3, 4)
+    far_relay("U", up_block)
     for copy in small:
         copy.wait_recv()
     biases()
     for k in range(8):
         yr[k].wait_recv()
-    to_sibling("A", group(0, 2, rows=UPPER))
+    to_sibling("B", group(0, 2, rows=UPPER))
     sibling_wait("A")
-    qkv(0)
+    whole(0)
+    qkv(0, 1 - yl)
     down_z(1)
+    whole(1)
+    qkv(1, 1 - yl)
+    sibling_wait("B")
+    qkv(0, yl)
+    third_pair(0)
+    up_y_send()
+    to_sibling("U", group(1, 0))
     windows(0)
     proj(0)
-    up_y_send()
-    to_sibling("U", group(1, 0))
-    qkv(1)
+    qkv(1, yl)
+    third_pair(1)
     down_z(2)
     windows(1)
     proj_relay(0)
@@ -578,11 +613,11 @@
     to_sibling("U", group(1, 1))
     to_sibling("U", group(1, -1))
     a_relay(0)
-    down_z(4)
-    norm_one(1)
     yr["U", 0].wait_recv()
     yr["U", 1].wait_recv()
     to_sibling("U", group(1, 2))
+    down_z(4)
+    norm_one(1)
     sibling_wait("U")
     up(0)
     a_relay(1)
@@ -590,13 +625,19 @@
     sibling_wait("D")
     down(0)
     up(1)
-    down_relay(0)
+    down_relay(0, 0)
+    down_relay(0, 1)
     down(1)
-    v0 = stats(0)
-    down_relay(1)
-    final(0, v0)
-    v1 = stats(1)
-    final(1, v1)
+    v0 = [stats(0, c) for c in range(2)]
+    for c in range(2):
+        down_relay(1, c)
+    kept = residual(0)
+    for c in range(2):
+        final(0, c, v0[c], *kept)
+    kept = residual(1)
+    v1 = [stats(1, c) for c in range(2)]
+    for c in range(2):
+        final(1, c, v1[c], *kept)
     for cp in oc:
         cp.wait_recv()
     for cp in started:
@@ -626,9 +667,10 @@
             pltpu.VMEM((3, 2, 2, NZ, 2, ROWS, PACK), BF),
             pltpu.VMEM((2, 2, PIECE, 128), BF),
             pltpu.VMEM((2, TOK, D), BF),
-            pltpu.VMEM((3, TOK, 128), BF),
-            pltpu.VMEM((3, TOK, 128), BF),
-            pltpu.VMEM((3, TOK, 128), BF),
+            pltpu.VMEM((2, 3, TOK, 128), BF),
+            pltpu.VMEM((2, 3, TOK, 128), BF),
+            pltpu.VMEM((2, 3, TOK, 128), BF),
+            pltpu.VMEM((2, 2, 2, TOK, 128), F32),
             pltpu.VMEM((2, TOK, 256), BF),
             pltpu.VMEM((2, TOK, D), BF),
             pltpu.VMEM((2, 2, 64, 768), BF),
@@ -638,8 +680,8 @@
             pltpu.VMEM((2, 4, PIECE, TOK), BF),
             pltpu.VMEM((2, 2, PART, TOK), BF),
             pltpu.VMEM((2, 2, PIECE, TOK), BF),
-            pltpu.VMEM((2, 8, TOK), F32),
-            pltpu.VMEM((2, 3, 8, TOK), F32),
+            pltpu.VMEM((2, 2, 8, 128), F32),
+            pltpu.VMEM((2, 2, 3, 8, 128), F32),
             pltpu.VMEM((2, 8, D), F32),
             pltpu.VMEM((2, 8, 8, 128), F32),
             pltpu.VMEM((3, 64, 128), F32),

time: 109 us -> 102 us (0.936)
  Pallas kernels: 107 us -> 99.6 us
    pallas_call x1, Pallas kernels: 107 us -> 99.6 us  [body(): pl.pallas_call(kernel, out_shape=jax.ShapeDtypeStruct((2, 2, 2, PART, 128...]
where the time goes in v3:
time: 102 us
  Pallas kernels  99.6 us (98%)
  local copies, waits for them, and re-layouts  2.2 us (2%)
    pallas_call x1, Pallas kernels, body(): pl.pallas_call(kernel, out_shape=jax.ShapeDtypeStruct((2, 2, 2, PART, 128...  99.6 us

profile of v3, /device:TPU:1, one launch (start us, length us, event | category | flops | bytes accessed | tf_op | source)
XLA Modules:
  0.0 101.9 jit_solution(17974746092699951096)
XLA Ops:
  0.0 99.6 %block.1 = bf16[2,2,2,192,128]{4,3,2,1,0:T(8,128)(2,1)} custom-call(bf16[8,192,128]{2,1,0:T(8,128)(2,1)} %field.1, bf16[48,192]{1,0:T(8,128)(2,1)} %w_query.1, bf16[48,192]{1,0:T(8,128)(2,1)} %w_key.1, bf16[48,192]{1,0:T(8,128)(2,1)} %w_value.1, bf16[48,192]{1,0:T(8,128)(2,1)} %bitcast.14, bf16[48,768]{1,0:T(8,128)(2,1)} %w_up.1, bf16[48,768]{1,0:T(8,128)(2,1)} %bitcast.13, ...), custom_call_target="tpu_custom_call" | custom-call | tf_op jit(solution)/shard_map/block/pallas_call | solution.py:651
  99.6 1.2 %copy.13 = bf16[2,2,2,192,128]{3,4,2,1,0:T(8,128)(2,1)S(1)} copy(bf16[2,2,2,192,128]{4,3,2,1,0:T(8,128)(2,1)} %block.1) | data formatting | bytes 786432 | tf_op jit(solution)/shard_map/block/pallas_call | solution.py:651
  100.8 0.2 pad_maximum_fusion
  101.0 1.0 copy.15
  (2 shorter events, 0.1 us)

commit v4 on v3

--- a/solution.py
+++ b/solution.py
@@ -373,16 +373,16 @@
         vn[g, 2] = jnp.where(first, v0, pltpu.roll(v1, 64, 1)).astype(BF)
 
     def windows(g):
-        def window(w, carry):
-            rows = pl.ds(pl.multiple_of(w * 64, 64), 64)
+        def window(w):
+            rows = pl.ds(w * 64, 64)
             for pair, ((p0, h0), (p1, h1)) in enumerate(HEADS_OF):
                 qq = qn[g, pair, rows]
                 both = jnp.concatenate([qq * low_bf, qq * high_bf], axis=0)
                 s = nt(kn[g, pair, rows], both)
                 scale = jnp.where(low[0:1], ea[p0, 3 + h0, 0:1, :], ea[p1, 3 + h1, 0:1, :])
                 s = s * scale + bias[pair]
-                if g == 1:
-                    s = s + jnp.where(jnp.logical_and(yl == 1, w == 3), poles, 0.0)
+                if g == 1 and w == 3:
+                    s = s + jnp.where(yl == 1, poles, 0.0)
                 e = jnp.exp(s - jnp.max(s, axis=0, keepdims=True))
                 e = e * (1.0 / jnp.sum(e, axis=0, keepdims=True))
                 o = nn(e.T.astype(BF), vn[g, pair, rows])
@@ -392,10 +392,9 @@
                 else:
                     at[0, rows, 0:128] = jnp.where(low, 0.0, pltpu.roll(o, 64, 1)).astype(BF)
                     at[1, rows, 0:128] = jnp.where(low, 0.0, o).astype(BF)
-            return carry
 
         for w in range(4):
-            window(w, 0)
+            window(w)
 
     def x_rows(dx):
         return pl.ds(pl.multiple_of(((x + dx + NX) % NX) * 64, 64), 64)
@@ -404,16 +403,16 @@
     pc = {}
 
     def proj(g):
-        def columns(n, carry):
+        def columns(n):
             total = None
             for part in range(2):
                 w = gw[0, part, n // 2, pl.ds((n % 2) * 4, 4), :, :, 512:768].reshape(PIECE, 256)
                 term = nt(at[part], w)
                 total = term if total is None else total + term
-            pb[g, :, pl.ds(pl.multiple_of(n * PIECE, 128), PIECE)] = total.astype(BF)
-            return carry
-
-        lax.fori_loop(0, 4, columns, 0)
+            pb[g, :, pl.ds(n * PIECE, PIECE)] = total.astype(BF)
+
+        for n in range(4):
+            columns(n)
         pc[g, "l", 1] = push(pb.at[g, x_rows(2), LEFT], rl.at[g, 0], at_x(1))
         pc[g, "l", -1] = push(pb.at[g, x_rows(2), RIGHT], rl.at[g, 1], at_x(-1))
         pc[g, "n", 1] = push(pb.at[g, x_rows(1), RIGHT], rp.at[g, 0, :, RIGHT], at_x(1))
@@ -457,14 +456,12 @@
             ac[g, sign, 1].wait_recv()
             ar[g, sign].wait_recv()
 
-        def columns(n, carry):
-            lo = pl.multiple_of((n % 3) * 256, 256)
-            w = gw[1, n // 3, :, :, :, :, pl.ds(lo, 256)].reshape(D, 256)
-            v = by_column(gelu(nn(af[g], w))).astype(BF)
-            hs[:, pl.ds(pl.multiple_of(n * 256, 256), 256)] = v
-            return carry
-
-        lax.fori_loop(0, 6, columns, 0)
+        def columns(n):
+            w = gw[1, n // 3, :, :, :, :, pl.ds((n % 3) * 256, 256)].reshape(D, 256)
+            hs[:, pl.ds(n * 256, 256)] = by_column(gelu(nn(af[g], w))).astype(BF)
+
+        for n in range(6):
+            columns(n)
 
     TOP, BOTTOM = pl.ds(0, PART), pl.ds(PART, PART)
     rc = {}
@@ -546,7 +543,6 @@
         yc["first", dy] = share(wblock(0, y, z, LOWER), at_y(dy))
     input_send(0)
     y_send(0)
-    small = tables()
     ss[...] = jnp.zeros_like(ss)
     far_relay("upper", upper)
     for dy in (1, -1, 2):
@@ -573,6 +569,7 @@
     lower_wait(1, -1)
     lower_to_sibling(1, -1)
     y_relay(5, 6, 7)
+    small = tables()
     down_y_send()
     to_sibling("A", group(0, 1, rows=UPPER))
     to_sibling("A", group(0, -1, rows=UPPER))
@@ -580,9 +577,6 @@
     lower_to_sibling(3, -3, 4)
     x_relay(1)
     far_relay("U", up_block)
-    for copy in small:
-        copy.wait_recv()
-    biases()
     for k in range(8):
         yr[k].wait_recv()
     to_sibling("B", group(0, 2, rows=UPPER))
@@ -597,6 +591,9 @@
     third_pair(0)
     up_y_send()
     to_sibling("U", group(1, 0))
+    for copy in small:
+        copy.wait_recv()
+    biases()
     windows(0)
     proj(0)
     qkv(1, yl)

time: 102 us -> 102 us (level)
  no operation moved by 1% of the time
where the time goes in v4:
time: 102 us
  Pallas kernels  99.2 us (97%)
  local copies, waits for them, and re-layouts  2.2 us (2%)
    pallas_call x1, Pallas kernels, body(): pl.pallas_call(kernel, out_shape=jax.ShapeDtypeStruct((2, 2, 2, PART, 128...  99.2 us

profile of v4, /device:TPU:1, one launch (start us, length us, event | category | flops | bytes accessed | tf_op | source)
XLA Modules:
  0.0 101.6 jit_solution(16004835528054408172)
XLA Ops:
  0.0 99.2 %block.1 = bf16[2,2,2,192,128]{4,3,2,1,0:T(8,128)(2,1)} custom-call(bf16[8,192,128]{2,1,0:T(8,128)(2,1)} %field.1, bf16[48,192]{1,0:T(8,128)(2,1)} %w_query.1, bf16[48,192]{1,0:T(8,128)(2,1)} %w_key.1, bf16[48,192]{1,0:T(8,128)(2,1)} %w_value.1, bf16[48,192]{1,0:T(8,128)(2,1)} %bitcast.14, bf16[48,768]{1,0:T(8,128)(2,1)} %w_up.1, bf16[48,768]{1,0:T(8,128)(2,1)} %bitcast.13, ...), custom_call_target="tpu_custom_call" | custom-call | tf_op jit(solution)/shard_map/block/pallas_call | solution.py:648
  99.2 1.2 %copy.13 = bf16[2,2,2,192,128]{3,4,2,1,0:T(8,128)(2,1)S(1)} copy(bf16[2,2,2,192,128]{4,3,2,1,0:T(8,128)(2,1)} %block.1) | data formatting | bytes 786432 | tf_op jit(solution)/shard_map/block/pallas_call | solution.py:648
  100.5 0.2 pad_maximum_fusion
  100.6 1.0 copy.15
  (2 shorter events, 0.1 us)

commit v5 on v4

--- a/solution.py
+++ b/solution.py
@@ -15,7 +15,7 @@
 TOK = 256
 PART = 192
 PIECE = 384
-SEMS = 224
+SEMS = 240
 
 
 def nt(a, b):
@@ -154,16 +154,16 @@
 
     ORDER = [0, 1, -1, 2, -2, 3, -3, 4]
 
-    def y_send_one(k):
-        ref = wblock(0, y, z + ORDER[k] + NZ, UPPER)
-        yc[k, 1] = share(ref, at_y(1))
-        yc[k, -1] = share(ref, at_y(-1))
-
-    def y_relay_one(k):
-        yc[k, 1].wait_recv()
-        yc[k, -1].wait_recv()
+    def y_send_one(k, t, rows):
+        ref = wblock(t, y, z + ORDER[k] + NZ, rows)
+        yc[t, k, 1] = share(ref, at_y(1))
+        yc[t, k, -1] = share(ref, at_y(-1))
+
+    def y_relay_one(k, t, rows):
+        yc[t, k, 1].wait_recv()
+        yc[t, k, -1].wait_recv()
         sign = 1 if k % 2 == 0 else -1
-        yr[k] = share(wblock(0, (y - sign + NY) % NY, z + ORDER[k] + NZ, UPPER), at_y(sign))
+        yr[t, k] = share(wblock(t, (y - sign + NY) % NY, z + ORDER[k] + NZ, rows), at_y(sign))
 
     def group(t, dy, zs=pl.ds(0, NZ), rows=pl.ds(0, ROWS)):
         yy = (y + dy + NY) % NY
@@ -189,13 +189,15 @@
         for dz in steps:
             zc[key, dz].wait_recv()
 
-    def y_send(*ks):
+    def y_send(*ks, t=0, rows=UPPER):
         for k in ks:
-            y_send_one(k)
-
-    def y_relay(*ks):
+            y_send_one(k, t, rows)
+
+    def y_relay(*ks, t=0, rows=UPPER):
         for k in ks:
-            y_relay_one(k)
+            y_relay_one(k, t, rows)
+
+    ALL = pl.ds(0, ROWS)
 
     def lower_to_sibling(*steps):
         for dz in steps:
@@ -210,22 +212,8 @@
         for part in range(2):
             far_wait(("lower", part), *steps)
 
-    HALVES = (pl.ds(0, 4), pl.ds(4, 4))
-
     def up_block(dz):
         return wblock(1, y, z + dz + NZ)
-
-    def up_y_send():
-        far_wait("U", 1, -1, 3, -3, 4)
-        for half in range(2):
-            for sign in (1, -1):
-                yc["U", half, sign] = share(group(1, 0, HALVES[half]), at_y(sign))
-
-    def up_y_relay(half):
-        yc["U", half, 1].wait_recv()
-        yc["U", half, -1].wait_recv()
-        sign = 1 - 2 * half
-        yr["U", half] = share(group(1, -sign, HALVES[half]), at_y(sign))
 
     def down_y_send():
         for dy in (1, -1, 2):
@@ -353,17 +341,14 @@
             xr[g, sign].wait_recv()
 
     def qkv(g, part):
-        def product(lo, size):
-            w = gw[0, part, :, :, :, :, lo:lo + size].reshape(D, size)
-            return nn(xf[g], w).astype(BF).astype(F32)
-
-        r = unit(product(0, 256))
+        w = gw[0, part, :, :, :, :, 0:640].reshape(D, 640)
+        v = nn(xf[g], w).astype(BF).astype(F32)
+        r = unit(v[:, :256])
         qn[g, part] = r[:, :128].astype(BF)
         kn[g, part] = r[:, 128:].astype(BF)
-        r = product(256, 256)
-        vn[g, part] = r[:, :128].astype(BF)
-        third[g, part, 0] = unit(r[:, 128:])
-        third[g, part, 1] = product(512, 128)
+        vn[g, part] = v[:, 256:384].astype(BF)
+        third[g, part, 0] = unit(v[:, 384:512])
+        third[g, part, 1] = v[:, 512:]
 
     def third_pair(g):
         first = lax.broadcasted_iota(jnp.int32, (TOK, 128), 1) < 64
@@ -385,7 +370,7 @@
                     s = s + jnp.where(yl == 1, poles, 0.0)
                 e = jnp.exp(s - jnp.max(s, axis=0, keepdims=True))
                 e = e * (1.0 / jnp.sum(e, axis=0, keepdims=True))
-                o = nn(e.T.astype(BF), vn[g, pair, rows])
+                o = nn(e.astype(BF).T, vn[g, pair, rows])
                 o = jnp.where(low, o[:64], o[64:])
                 if pair < 2:
                     at[pair, rows, 128:256] = o.astype(BF)
@@ -571,6 +556,7 @@
     y_relay(5, 6, 7)
     small = tables()
     down_y_send()
+    y_send(0, t=1, rows=ALL)
     to_sibling("A", group(0, 1, rows=UPPER))
     to_sibling("A", group(0, -1, rows=UPPER))
     lower_wait(3, -3, 4)
@@ -578,40 +564,43 @@
     x_relay(1)
     far_relay("U", up_block)
     for k in range(8):
-        yr[k].wait_recv()
+        yr[0, k].wait_recv()
     to_sibling("B", group(0, 2, rows=UPPER))
+    far_wait("U", 1, -1)
+    y_send(1, 2, 3, 4, t=1, rows=ALL)
     sibling_wait("A")
     whole(0)
     qkv(0, 1 - yl)
-    down_z(1)
     whole(1)
     qkv(1, 1 - yl)
+    down_z(1)
     sibling_wait("B")
     qkv(0, yl)
     third_pair(0)
-    up_y_send()
-    to_sibling("U", group(1, 0))
     for copy in small:
         copy.wait_recv()
     biases()
+    far_wait("U", 3, -3, 4)
+    y_send(5, 6, 7, t=1, rows=ALL)
+    to_sibling("U", group(1, 0))
     windows(0)
     proj(0)
     qkv(1, yl)
     third_pair(1)
+    windows(1)
     down_z(2)
-    windows(1)
     proj_relay(0)
     proj(1)
-    up_y_relay(0)
+    y_relay(0, 1, 2, 3, 4, t=1, rows=ALL)
     norm_one(0)
-    down_z(3)
     proj_relay(1)
-    up_y_relay(1)
+    y_relay(5, 6, 7, t=1, rows=ALL)
     to_sibling("U", group(1, 1))
     to_sibling("U", group(1, -1))
+    down_z(3)
     a_relay(0)
-    yr["U", 0].wait_recv()
-    yr["U", 1].wait_recv()
+    for k in range(8):
+        yr[1, k].wait_recv()
     to_sibling("U", group(1, 2))
     down_z(4)
     norm_one(1)

time: 102 us -> 100 us (0.980)
  Pallas kernels: 99.2 us -> 97.5 us
    pallas_call x1, Pallas kernels: 99.2 us -> 97.5 us  [body(): pl.pallas_call(kernel, out_shape=jax.ShapeDtypeStruct((2, 2, 2, PART, 128...]
where the time goes in v5:
time: 100 us; the launch traced here: 99.9 us
  Pallas kernels  97.5 us (98%)
  local copies, waits for them, and re-layouts  2.2 us (2%)
    pallas_call x1, Pallas kernels, body(): pl.pallas_call(kernel, out_shape=jax.ShapeDtypeStruct((2, 2, 2, PART, 128...  97.5 us

profile of v5, /device:TPU:1, one launch (start us, length us, event | category | flops | bytes accessed | tf_op | source)
XLA Modules:
  0.0 99.9 jit_solution(2703760910185081938)
XLA Ops:
  0.0 97.5 %block.1 = bf16[2,2,2,192,128]{4,3,2,1,0:T(8,128)(2,1)} custom-call(bf16[8,192,128]{2,1,0:T(8,128)(2,1)} %field.1, bf16[48,192]{1,0:T(8,128)(2,1)} %w_query.1, bf16[48,192]{1,0:T(8,128)(2,1)} %w_key.1, bf16[48,192]{1,0:T(8,128)(2,1)} %w_value.1, bf16[48,192]{1,0:T(8,128)(2,1)} %bitcast.14, bf16[48,768]{1,0:T(8,128)(2,1)} %w_up.1, bf16[48,768]{1,0:T(8,128)(2,1)} %bitcast.13, ...), custom_call_target="tpu_custom_call" | custom-call | tf_op jit(solution)/shard_map/block/pallas_call | solution.py:637
  97.6 1.2 %copy.13 = bf16[2,2,2,192,128]{3,4,2,1,0:T(8,128)(2,1)S(1)} copy(bf16[2,2,2,192,128]{4,3,2,1,0:T(8,128)(2,1)} %block.1) | data formatting | bytes 786432 | tf_op jit(solution)/shard_map/block/pallas_call | solution.py:637
  98.8 0.2 pad_maximum_fusion
  99.0 1.0 copy.15
  (2 shorter events, 0.1 us)

commit v6 on v5

--- a/solution.py
+++ b/solution.py
@@ -38,7 +38,7 @@
 def kernel(
     field, w_query, w_key, w_value, w_proj, w_up, w_down, logit, rel, g_attn, g_mlp, out,
     fr, rq, rk, rv, rpj, sc, tb, rga, rgm,
-    blk, gw, rin, xf, qn, kn, vn, third, at, pb, rl, rp, af, hs, db, rdl, rd, ss, st, ga, ea, bias, ob,
+    blk, gw, rin, xf, qn, kn, vn, third, at, pb, rl, rp, af, hs, db, rdl, rd, ss, st, ga, ea, bias, ob, oin,
     load, send, recv,
 ):
     lon = lax.axis_index("lon")
@@ -517,11 +517,11 @@
         o = res[:, c * 128:c * 128 + 128] + (v - mean) * lax.rsqrt(var + 1e-5) * gains
         ob[g, c] = o.astype(BF).reshape(2, PART, 128)
         if c == 0:
-            out[yl, g, 1] = ob[g, 0, yl]
-            oc.append(push(ob.at[g, 0, 1 - yl], out.at[yl, g, 1], partner))
+            oin[yl, g, 1] = ob[g, 0, yl]
+            oc.append(push(ob.at[g, 0, 1 - yl], oin.at[yl, g, 1], partner))
         else:
-            oc.append(push(ob.at[g, 1, 1 - yl], out.at[yl, g, 0], at_lon(1, 1)))
-            oc.append(push(ob.at[g, 1, yl], out.at[yl, g, 0], at_lon(1, 0)))
+            oc.append(push(ob.at[g, 1, 1 - yl], oin.at[yl, g, 0], at_lon(1, 1)))
+            oc.append(push(ob.at[g, 1, yl], oin.at[yl, g, 0], at_lon(1, 0)))
 
     far_send("upper", upper)
     for dy in (1, -1, 2):
@@ -626,6 +626,22 @@
         final(1, c, v1[c], *kept)
     for cp in oc:
         cp.wait_recv()
+
+    quarter = (lax.broadcasted_iota(jnp.int32, (32, 128), 1) + 124) % 128 // 32
+
+    def ungroup(i, carry):
+        rows = pl.ds(pl.multiple_of(i * 32, 32), 32)
+        for side in range(2):
+            parts = [oin[k // 2, k % 2, side, rows, :].astype(F32) for k in range(4)]
+            for j in range(4):
+                v = None
+                for k in range(4):
+                    moved = pltpu.roll(parts[k], (32 * (k - j) + 4) % 128, 1)
+                    v = moved if v is None else jnp.where(quarter == k, moved, v)
+                out[side * 4 + j, rows, :] = v.astype(BF)
+        return carry
+
+    lax.fori_loop(0, PART // 32, ungroup, 0)
     for cp in started:
         cp.wait_send()
 
@@ -634,9 +650,9 @@
     field, w_query, w_key, w_value, w_proj, w_up, w_down, logit_scale, rel_bias, gain_attn, gain_mlp
 ):
     anywhere = pl.BlockSpec(memory_space=pl.ANY)
-    out = pl.pallas_call(
+    return pl.pallas_call(
         kernel,
-        out_shape=jax.ShapeDtypeStruct((2, 2, 2, PART, 128), BF),
+        out_shape=jax.ShapeDtypeStruct((8, PART, 128), BF),
         in_specs=[anywhere] * 11,
         out_specs=pl.BlockSpec(memory_space=pltpu.VMEM),
         scratch_shapes=[
@@ -672,6 +688,7 @@
             pltpu.VMEM((2, 8, 8, 128), F32),
             pltpu.VMEM((3, 64, 128), F32),
             pltpu.VMEM((2, 2, 2, PART, 128), BF),
+            pltpu.VMEM((2, 2, 2, PART, 128), BF),
             pltpu.SemaphoreType.DMA((11,)),
             pltpu.SemaphoreType.DMA((SEMS,)),
             pltpu.SemaphoreType.DMA((SEMS,)),
@@ -684,8 +701,6 @@
         field, w_query, w_key, w_value, w_proj.T, w_up, w_down.T,
         logit_scale.reshape(1, 3), rel_bias, gain_attn.reshape(1, PART), gain_mlp.reshape(1, PART),
     )
-    mixed = out.reshape(2, 2, 2, PART, 4, 32).transpose(2, 4, 3, 0, 1, 5)
-    return jnp.roll(mixed.reshape(8, PART, 128), 4, axis=2)
 
 
 def solution(mesh):

time: 100 us -> 100 us (level)
    unnamed x0 -> x1, local copies, waits for them, and re-layouts: none -> 1.77 us
    pallas_call x1 -> x0, local copies, waits for them, and re-layouts: 1.2 us -> none  [body(): pl.pallas_call(kernel, out_shape=jax.ShapeDtypeStruct((2, 2, 2, PART, 128...]
where the time goes in v6:
time: 100 us
  Pallas kernels  98.4 us (98%)
  local copies, waits for them, and re-layouts  1.77 us (2%)
    pallas_call x1, Pallas kernels, body(): pl.pallas_call(kernel, out_shape=jax.ShapeDtypeStruct((8, PART, 128), BF)...  98.4 us

profile of v6, /device:TPU:1, one launch (start us, length us, event | category | flops | bytes accessed | tf_op | source)
XLA Modules:
  0.0 100.2 jit_solution(8192248690585403856)
XLA Ops:
  0.0 98.4 %block.1 = bf16[8,192,128]{2,1,0:T(8,128)(2,1)} custom-call(bf16[8,192,128]{2,1,0:T(8,128)(2,1)} %field.1, bf16[48,192]{1,0:T(8,128)(2,1)} %w_query.1, bf16[48,192]{1,0:T(8,128)(2,1)} %w_key.1, bf16[48,192]{1,0:T(8,128)(2,1)} %w_value.1, bf16[48,192]{1,0:T(8,128)(2,1)} %bitcast.6, bf16[48,768]{1,0:T(8,128)(2,1)} %w_up.1, bf16[48,768]{1,0:T(8,128)(2,1)} %bitcast.5, ...), custom_call_target="tpu_custom_call" | custom-call | tf_op jit(solution)/shard_map/block/pallas_call | solution.py:653
  98.4 1.8 %copy.13 = bf16[8,192,128]{2,1,0:T(8,128)(2,1)} copy(bf16[8,192,128]{2,1,0:T(8,128)(2,1)} %block.1) | data formatting | bytes 786432
